TPU v7x, 512 devices: a whole 4x8x8 slice. The times are simulated.
512 devices in a mesh: dap: 128 (over x, z_hi, y), seq: 4 (over z_lo, core).
Axes of the slice: x: 4, y: 8, z: 8 (z_hi: 4, z_lo: 2; z = z_hi * 2 + z_lo), core: 2. Of those that a mesh axis runs over, the one named last changes fastest.
Arguments:
- homolog_stack: bfloat16 [256, 512, 256], P('seq', 'dap'), may hold values from -8 to 8
- homolog_existing_flags: int32 [256], replicated, may hold values 0 or 1
- amino_existing_flags: int32 [512], replicated, may hold values 0 or 1
- asking_weights: bfloat16 [256, 256], replicated, may hold values from -16 to 16
- lookup_weights: bfloat16 [256, 256], replicated, may hold values from -1 to 1
- content_weights: bfloat16 [256, 256], replicated, may hold values from -0.375 to 0.375
- sigmoid_weights: bfloat16 [256, 256], replicated, may hold values from -0.375 to 0.375
- final_projection: bfloat16 [256, 256], replicated, may hold values from -0.375 to 0.375
- former_weights: bfloat16 [256, 32], replicated, may hold values from -0.375 to 0.375
- latter_weights: bfloat16 [256, 32], replicated, may hold values from -0.375 to 0.375
- couple_projection: float32 [1024, 128], replicated, may hold values from -3 to 3
Outputs:
- attended_homologs: bfloat16 [256, 512, 256], P('seq', 'dap')
- pair_increment: bfloat16 [512, 512, 128], P('dap', 'seq')
All inputs are finite; a program needn't handle non-finite values.
Results may differ from a plain program's by a relative error of at most 0.015.
Values may be sent and summed in bfloat16 or wider, within the bound.
A program may use at most 64 MiB of HBM per device.

v0:
```python
import jax
import jax.numpy as jnp
from jax import lax
from jax.sharding import PartitionSpec as P

HEADS = 8
PER_HEAD_DIM = 32
PROJECTED_DIM = 32
PAIR = 128


def standard_rescale(values):
    mean = jnp.mean(values, axis=-1, keepdims=True)
    centred = values - mean
    variance = jnp.mean(centred * centred, axis=-1, keepdims=True)
    return centred * lax.rsqrt(variance + 1e-05)


def project(flat_rows, weight):
    return jnp.dot(flat_rows, weight, preferred_element_type=jnp.float32)


def contract(left_part, right_part, couple_projection):
    outer = jnp.einsum("sic,sje->ijce", left_part, right_part, preferred_element_type=jnp.float32)
    rows_here = outer.shape[0]
    cols_here = outer.shape[1]
    flat_outer = outer.reshape(rows_here * cols_here, PROJECTED_DIM * PROJECTED_DIM)
    return jnp.dot(flat_outer, couple_projection, precision=lax.Precision.HIGHEST).reshape(
        rows_here, cols_here, PAIR
    )


def on_device(
    homolog_stack,
    homolog_existing_flags,
    amino_existing_flags,
    asking_weights,
    lookup_weights,
    content_weights,
    sigmoid_weights,
    final_projection,
    former_weights,
    latter_weights,
    couple_projection,
):
    homolog_entries, amino_positions, feature_extent = homolog_stack.shape
    incoming_tensor = homolog_stack.astype(jnp.float32)
    rescaled_stack = standard_rescale(incoming_tensor).astype(jnp.bfloat16)
    flattened_view = rescaled_stack.reshape(homolog_entries * amino_positions, feature_extent)
    query = (project(flattened_view, asking_weights) * PER_HEAD_DIM ** (-0.5)).astype(jnp.bfloat16)
    query = query.reshape(homolog_entries, amino_positions, HEADS, PER_HEAD_DIM)
    gate = jax.nn.sigmoid(project(flattened_view, sigmoid_weights))
    keys_here = (
        project(flattened_view, lookup_weights)
        .astype(jnp.bfloat16)
        .reshape(homolog_entries, amino_positions, feature_extent)
    )
    values_here = (
        project(flattened_view, content_weights)
        .astype(jnp.bfloat16)
        .reshape(homolog_entries, amino_positions, feature_extent)
    )
    keys_all, values_all = (
        lax.all_gather(keys_here, "seq", axis=0, tiled=True),
        lax.all_gather(values_here, "seq", axis=0, tiled=True),
    )
    keys_all = keys_all.reshape(-1, amino_positions, HEADS, PER_HEAD_DIM)
    values_all = values_all.reshape(-1, amino_positions, HEADS, PER_HEAD_DIM)
    scores = jnp.einsum("sihd,tihd->ihst", query, keys_all, preferred_element_type=jnp.float32)
    scores = jnp.where((homolog_existing_flags > 0)[None, None, None, :], scores, -1000000000.0)
    weights = jax.nn.softmax(scores, axis=-1).astype(jnp.bfloat16)
    weighted_mix = jnp.einsum(
        "ihst,tihd->sihd", weights, values_all, preferred_element_type=jnp.float32
    )
    gated = (gate * weighted_mix.reshape(homolog_entries * amino_positions, feature_extent)).astype(
        jnp.bfloat16
    )
    carried_change = project(gated, final_projection)
    attended_homologs = (
        incoming_tensor + carried_change.reshape(homolog_entries, amino_positions, feature_extent)
    ).astype(jnp.bfloat16)
    latter_rescaled = (
        standard_rescale(attended_homologs.astype(jnp.float32))
        .astype(jnp.bfloat16)
        .reshape(homolog_entries * amino_positions, feature_extent)
    )
    seq_start = lax.axis_index("seq") * homolog_entries
    res_start = lax.axis_index("dap") * amino_positions
    rows_here = lax.dynamic_slice_in_dim(homolog_existing_flags, seq_start, homolog_entries).astype(
        jnp.float32
    )
    residues_here = lax.dynamic_slice_in_dim(
        amino_existing_flags, res_start, amino_positions
    ).astype(jnp.float32)
    present = rows_here[:, None] * residues_here[None, :]
    left = (
        project(latter_rescaled, former_weights).reshape(
            homolog_entries, amino_positions, PROJECTED_DIM
        )
        * present[:, :, None]
    ).astype(jnp.bfloat16)
    right = (
        project(latter_rescaled, latter_weights).reshape(
            homolog_entries, amino_positions, PROJECTED_DIM
        )
        * present[:, :, None]
    ).astype(jnp.bfloat16)
    partial_pair = contract(
        left, lax.all_gather(right, "dap", axis=1, tiled=True), couple_projection
    )
    projected = lax.psum_scatter(partial_pair, "seq", scatter_dimension=1, tiled=True)
    col_count = projected.shape[1]
    col_start = lax.axis_index("seq") * col_count
    residues_cols = lax.dynamic_slice_in_dim(amino_existing_flags, col_start, col_count).astype(
        jnp.float32
    )
    count = jnp.sum(homolog_existing_flags.astype(jnp.float32))
    norm = count * residues_here[:, None] * residues_cols[None, :]
    pair_increment = (projected / jnp.maximum(norm, 1.0)[:, :, None]).astype(jnp.bfloat16)
    return (attended_homologs, pair_increment)


def solution(mesh):
    in_specs = (P("seq", "dap", None), P(), P(), P(), P(), P(), P(), P(), P(), P(), P())
    out_specs = (P("seq", "dap", None), P("dap", "seq", None))
    return jax.shard_map(
        on_device, mesh=mesh, in_specs=in_specs, out_specs=out_specs, check_vma=False
    )
```

profile of v0, /device:TPU:1, one launch (start us, length us, event | category | flops | bytes accessed | tf_op | source)
XLA Modules:
  0.0 241.8 jit_solution(18359766687316473535)
XLA Ops:
  7.2 0.7 broadcast_compare_fusion
  8.0 1.3 convert_reduce_fusion.2
  9.3 1.0 convert_reduce_fusion
  10.3 1.2 fusion.27
  11.5 1.1 fusion.28
  12.7 1.1 convolution_convert_fusion
  13.8 13.2 %all_gather.10 = bf16[256,4,256]{2,1,0:T(4,128)(2,1)S(1)} all-gather(bf16[64,4,256]{2,1,0:T(4,128)(2,1)S(1)} %reshape.126), channel_id=1, replica_groups=mesh['dap'=128,'seq'=4] {'seq'}, dimensions={0}, use_global_device_ids=true | all-gather | bytes 655360 | tf_op jit(solution)/shard_map/all_gather | solution.py:64
  27.1 0.3 copy.25
  27.6 0.2 reshape.125
  28.1 7.3 %all_gather.9 = bf16[256,4,256]{2,1,0:T(4,128)(2,1)S(1)} all-gather(bf16[64,4,256]{2,1,0:T(4,128)(2,1)S(1)} %reshape.123), channel_id=1, replica_groups=mesh['dap'=128,'seq'=4] {'seq'}, dimensions={0}, use_global_device_ids=true | all-gather | bytes 655360 | tf_op jit(solution)/shard_map/all_gather | solution.py:65
  35.4 0.3 copy.24
  35.7 0.8 fusion.60
  36.5 3.7 %convolution_bitcast_fusion = f32[64,4,8,32]{0,3,2,1:T(8,128)S(1)} fusion(bf16[256,4,8,32]{0,3,2,1:T(8,128)(2,1)S(1)} %bitcast.41, f32[4,8,64]{2,1,0:T(8,128)S(1)} %fusion.60, pred[256]{0:T(512)(128)(4,1)S(1)} %broadcast_compare_fusion, bf16[256,4,8,32]{0,3,2,1:T(8,128)(2,1)S(1)} %bitcast.40, bf16[64,4,8,32]{3,2,1,0:T(8,128)(2,1)S(1)} %reshape.125), kind=kOutput, calls=%fused_computation.8 | convolution fusion | flops 69208320 | bytes 1450240 | tf_op jit(solution)/shard_map/ihst,tihd->sihd/dot_general | solution.py:72
  40.2 0.9 copy.27
  41.2 0.3 reshape.128
  41.5 0.3 fusion.13
  42.7 0.7 broadcast_multiply_fusion.3
  43.5 0.8 fusion.14
  44.6 129.7 %all-gather.2.cloned.1.call-done = bf16[64,512,32]{0,2,1:T(8,128)(2,1)} async-done(((bf16[64,4,32]{0,2,1:T(8,128)(2,1)}), bf16[64,512,32]{0,2,1:T(8,128)(2,1)}) %all-gather.2.cloned.1.call-update) | async-done | bytes 2097168 | tf_op jit(solution)/shard_map/all_gather | solution.py:109
  174.3 10.3 %fusion.3 = f32[4,512,32,32]{1,2,0,3:T(8,128)} fusion(bf16[64,512,32,1]{0,2,1,3:T(8,128)(2,1)} %bitcast.38, bf16[64,4,256]{2,1,0:T(4,128)(2,1)S(1)} %fusion.30, f32[64,4]{0,1:T(4,128)S(1)} %broadcast_multiply_fusion.2, bf16[256,32]{0,1:T(8,128)(2,1)S(1)} %copy-done.5), kind=kOutput, calls=%fused_computation.3 | convolution fusion | flops 272646144 | bytes 10634240 | tf_op jit(solution)/shard_map/sic,sje->ijce/dot_general | solution.py:24
  184.6 8.2 %copy.31 = f32[4,512,32,32]{1,3,2,0:T(8,128)S(1)} copy(f32[4,512,32,32]{1,2,0,3:T(8,128)} %fusion.3) | data formatting | bytes 16777216 | tf_op jit(solution)/shard_map/sic,sje->ijce/transpose | solution.py:24
  192.9 15.0 %fusion.19 = f32[4,512,128]{2,1,0:T(8,128)} fusion(f32[4,512,1024]{1,2,0:T(8,128)S(1)} %bitcast.37, f32[1024,128]{1,0:T(8,128)S(1)} %copy-done), kind=kOutput, calls=%fused_computation.27 | convolution fusion | flops 3221225472 | bytes 9961472 | tf_op jit(solution)/shard_map/dot_general | solution.py:28
  208.0 25.2 %reduce-scatter.2.cloned.1.call-done = f32[4,128,128]{2,1,0:T(8,128)} async-done(((f32[4,512,128]{2,1,0:T(8,128)}), f32[4,128,128]{2,1,0:T(8,128)}) %reduce-scatter.2.cloned.1.call-update) | async-done | bytes 262160 | tf_op jit(solution)/shard_map/reduce_scatter | solution.py:111
  233.2 1.7 divide_convert_fusion.2
  (43 shorter events, 1.9 us)
Async XLA Ops:
  7.2 185.7 %copy-start = (f32[1024,128]{1,0:T(8,128)S(1)}, f32[1024,128]{1,0:T(8,128)}, u32[]{:S(2)}) copy-start(f32[1024,128]{1,0:T(8,128)} %param.21) | copy-start | bytes 1572868
  7.2 20.2 %copy-start.3 = (bf16[256,256]{1,0:T(8,128)(2,1)S(1)}, bf16[256,256]{1,0:T(8,128)(2,1)}, u32[]{:S(2)}) copy-start(bf16[256,256]{1,0:T(8,128)(2,1)} %param.14) | copy-start | bytes 393220
  7.2 167.1 %all-gather.2.cloned.1.call-start = ((), (), s32[]{:S(2)}) async-start(), calls=%async_computation.1 | async-start | bytes 4227072 | tf_op jit(solution)/shard_map/all_gather | solution.py:109
  10.3 17.5 %copy-start.4 = (bf16[256,256]{1,0:T(8,128)(2,1)S(1)}, bf16[256,256]{1,0:T(8,128)(2,1)}, u32[]{:S(2)}) copy-start(bf16[256,256]{1,0:T(8,128)(2,1)} %param.16) | copy-start | bytes 393220
  40.2 1.3 copy-start.7
  40.2 1.3 copy-start.8
  40.2 1.8 copy-start.1
  41.2 1.5 copy-start.10
  41.2 1.6 copy-start.6
  41.2 2.4 copy-start.9
  41.2 133.1 %copy-start.5 = (bf16[256,32]{0,1:T(8,128)(2,1)S(1)}, bf16[256,32]{0,1:T(8,128)(2,1)}, u32[]{:S(2)}) copy-start(bf16[256,32]{0,1:T(8,128)(2,1)} %param.19) | copy-start | bytes 49156
  42.1 142.5 %copy-start.2 = (bf16[64,4,256]{2,1,0:T(4,128)(2,1)}, bf16[64,4,256]{2,1,0:T(4,128)(2,1)S(1)}, u32[]{:S(2)}) copy-start(bf16[64,4,256]{2,1,0:T(4,128)(2,1)S(1)} %get-tuple-element.5) | copy-start | bytes 393220
  44.3 188.8 %reduce-scatter.2.cloned.1.call-start = ((), (), s32[]{:S(2)}) async-start(), calls=%async_computation.2 | async-start | bytes 1310720 | tf_op jit(solution)/shard_map/reduce_scatter | solution.py:111
Sparse Core Ops, SparseCore 0:
  44.5 129.7 all-gather.1
  208.0 25.1 reduce-scatter.1
where the time goes:
time: 242 us
  waiting for transfers between devices  155 us (64%)
  matrix products  32.4 us (13%)
  blocking collectives  20.5 us (8%)
  between operations  14.4 us (6%)
  local copies, waits for them, and re-layouts  10.6 us (4%)
  other arithmetic  8.74 us (4%)
    all_gather x1, waiting for transfers between devices, on_device(): lax.all_gather(right, 'dap', axis=1, tiled=True)  130 us
    reduce_scatter x1, waiting for transfers between devices, on_device(): lax.psum_scatter(partial_pair, 'seq', scatter_dimension=1, tiled=True)  25.2 us
    dot_general x1, matrix products, contract(): jnp.dot(flat_outer, couple_projection, precision=lax.Precision.HIGHEST)  15 us
    all_gather x1, blocking collectives, on_device(): lax.all_gather(keys_here, 'seq', axis=0, tiled=True)  13.2 us
    dot_general x1, matrix products, contract(): jnp.einsum('sic,sje->ijce', left_part, right_part, preferred_element_type...  10.3 us
    transpose x1, local copies, waits for them, and re-layouts, contract(): jnp.einsum('sic,sje->ijce', left_part, right_part, preferred_element_type...  8.24 us
    all_gather x1, blocking collectives, on_device(): lax.all_gather(values_here, 'seq', axis=0, tiled=True)  7.29 us
  transfers between devices with their start and end apart: 2, of which 2 were waited for; matrix products, arithmetic and copies ran while one was open for 0% of the time, Pallas kernels for 0%

commit v1 on v0

v1 whole, which is shorter than its diff:
```python
import functools

import jax
import jax.numpy as jnp
from jax import lax
from jax.experimental import pallas as pl
from jax.experimental.pallas import tpu as pltpu
from jax.sharding import PartitionSpec as P

HEADS = 8
PER_HEAD_DIM = 32
PROJECTED_DIM = 32
PAIR = 128
FEATURES = 256
SEQS = 256
X, ZH, Y, SEQ = 4, 4, 8, 4
LEFTS = X * ZH
RIGHTS = Y * SEQ
MESH = pl.DeviceIdType.MESH
F32 = jnp.float32
BF16 = jnp.bfloat16


def dot(a, b):
    return lax.dot_general(a, b, (((1,), (0,)), ((), ())), preferred_element_type=F32)


def dot_t(a, b):
    return lax.dot_general(a, b, (((1,), (1,)), ((), ())), preferred_element_type=F32)


def eye(size):
    rows = lax.broadcasted_iota(jnp.int32, (size, size), 0)
    cols = lax.broadcasted_iota(jnp.int32, (size, size), 1)
    return jnp.where(rows == cols, 1.0, 0.0).astype(BF16)


def rescale_rows(values):
    mean = jnp.mean(values, axis=0, keepdims=True)
    centred = values - mean
    variance = jnp.mean(centred * centred, axis=0, keepdims=True)
    return centred * lax.rsqrt(variance + 1e-05)


def kernel(
    stack_ref, homolog_ref, amino_ref, amino_smem,
    asking_ref, lookup_ref, content_ref, sigmoid_ref, final_ref, former_ref, latter_ref, couple_ref,
    att_ref, pair_ref,
    stack_all, att_send, left_all, right_all, wt, wt_final, wt_pair, couple, key_mask,
    left_wide, outer, projected, tiles, norm_cols,
    stack_ss, stack_rs, att_ss, att_rs, left_ss, left_rs,
    right_ls, right_ys, right_fs, right_cs, right_rs, tile_ss, tile_rs,
):
    dap = lax.axis_index("dap")
    seq = lax.axis_index("seq")
    x, zh, y = lax.div(dap, ZH * Y), lax.rem(lax.div(dap, Y), ZH), lax.rem(dap, Y)
    l, c = lax.div(seq, 2), lax.rem(seq, 2)

    def dap_of(px, pzh, py):
        return (px * ZH + pzh) * Y + py

    def seq_peer(n):
        return lax.rem(seq + n, SEQ)

    def left_peer(n):
        return lax.rem(x + lax.div(n, ZH), X), lax.rem(zh + lax.rem(n, ZH), ZH)

    def y_peer(n):
        odd = lax.rem(n, 2)
        half = lax.div(n, 2)
        step = odd * (half + 1) + (1 - odd) * (Y - half)
        return lax.rem(y + step, Y)

    def copy_to(src, dst, send_sem, recv_sem, device):
        return pltpu.make_async_remote_copy(
            src_ref=src, dst_ref=dst, send_sem=send_sem, recv_sem=recv_sem,
            device_id=device, device_id_type=MESH,
        )

    def each(lo, hi, body):
        def step(n, carry):
            body(n)
            return carry
        lax.fori_loop(lo, hi, step, 0)

    barrier = pltpu.get_barrier_semaphore()

    def greet(device):
        pl.semaphore_signal(barrier, inc=1, device_id=device, device_id_type=MESH)

    each(1, SEQ, lambda n: greet((dap, seq_peer(n))))

    def greet_left(n):
        px, pzh = left_peer(n)
        greet((dap_of(px, pzh, y), seq))

    each(1, LEFTS, greet_left)
    each(1, Y, lambda n: greet((dap_of(x, zh, y_peer(n)), seq)))

    def greet_tile(n):
        greet((dap_of(seq, lax.rem(zh + lax.div(n, SEQ), ZH), y), lax.rem(seq + lax.rem(n, SEQ), SEQ)))

    each(1, ZH * SEQ, greet_tile)
    pl.when(x != seq)(lambda: greet_tile(0))

    ident = eye(FEATURES)
    for n, ref in enumerate((asking_ref, lookup_ref, content_ref, sigmoid_ref)):
        wt[n * FEATURES:(n + 1) * FEATURES, :] = dot_t(ident, ref[...]).astype(BF16)
    wt_final[...] = dot_t(ident, final_ref[...]).astype(BF16)
    wt_pair[:PROJECTED_DIM, :] = former_ref[...]
    wt_pair[PROJECTED_DIM:, :] = latter_ref[...]
    couple[...] = couple_ref[...].astype(BF16)
    flags = homolog_ref[...].astype(F32)
    diagonal = (ident.astype(F32) * flags).astype(BF16)
    key_mask[...] = dot(diagonal, jnp.ones((SEQS, SEQS), BF16))
    count = jnp.sum(flags, axis=1, keepdims=True)
    residues = amino_ref.shape[1]
    first_col = dap_of(x, zh, 0) * SEQ
    rows = lax.broadcasted_iota(jnp.int32, (RIGHTS, residues), 0)
    cols = lax.broadcasted_iota(jnp.int32, (RIGHTS, residues), 1)
    picked = jnp.where(cols == rows + first_col, 1.0, 0.0).astype(BF16)
    amino_wide = jnp.broadcast_to(amino_ref[...].astype(F32), (PAIR, residues)).astype(BF16)
    norm_cols[...] = dot_t(picked, amino_wide) * count
    amino_here = amino_smem[dap * SEQ + seq].astype(F32)

    greeted = SEQ - 1 + LEFTS - 1 + Y - 1 + ZH * SEQ
    pl.when(x != seq)(lambda: pl.semaphore_wait(barrier, greeted))
    pl.when(x == seq)(lambda: pl.semaphore_wait(barrier, greeted - 1))

    def stack_copy(n, slot):
        q = seq_peer(n)
        return copy_to(stack_ref.at[q], stack_all.at[slot], stack_ss.at[n], stack_rs.at[slot], (dap, q))

    each(1, SEQ, lambda n: stack_copy(n, seq).start())
    stack_all[seq] = stack_ref[seq]
    each(1, SEQ, lambda n: stack_copy(n, seq_peer(n)).wait_recv())

    incoming = dot_t(ident, stack_all[...].reshape(SEQS, FEATURES))
    normed = rescale_rows(incoming).astype(BF16)
    query = (dot(wt[0:256, :], normed) * PER_HEAD_DIM ** (-0.5)).astype(BF16)
    key_t = dot(wt[256:512, :], normed).astype(BF16)
    value = dot(wt[512:768, :], normed).astype(BF16)
    gate = jax.nn.sigmoid(dot(wt[768:1024, :], normed))
    key = dot_t(ident, key_t).astype(BF16)
    here = key_mask[...] > 0.5
    gated = []
    for h in range(HEADS):
        lo = h * PER_HEAD_DIM
        group = lo // 128 * 128
        before, after = lo - group, 128 - PER_HEAD_DIM - (lo - group)
        parts = [query[lo:lo + PER_HEAD_DIM]]
        if before:
            parts.insert(0, jnp.zeros((before, SEQS), BF16))
        if after:
            parts.append(jnp.zeros((after, SEQS), BF16))
        scores = dot(key[:, group:group + 128], jnp.concatenate(parts, axis=0))
        scores = jnp.where(here, scores, -1000000000.0)
        weights = jnp.exp(scores - jnp.max(scores, axis=0, keepdims=True))
        total = jnp.sum(weights, axis=0, keepdims=True)
        mixed = dot(value[lo:lo + PER_HEAD_DIM], weights.astype(BF16))
        gated.append((gate[lo:lo + PER_HEAD_DIM] * (mixed / total)).astype(BF16))
    gated = jnp.concatenate(gated, axis=0)
    attended = (incoming + dot(wt_final[...], gated)).astype(BF16)

    normed2 = rescale_rows(attended.astype(F32)).astype(BF16)
    sides = (dot(wt_pair[...], normed2) * (flags * amino_here)).astype(BF16)

    def right_slot(core, py, pl_):
        return core * (Y * 2) + py * 2 + pl_

    def right_copy(pl_, py, send_sem, device):
        slot = right_slot(c, py, pl_)
        return copy_to(right_all.at[slot], right_all.at[slot], send_sem, right_rs.at[slot], device)

    def right_arrived(slot):
        copy_to(right_all.at[slot], right_all.at[slot], right_ls.at[0], right_rs.at[slot], (dap, seq)).wait_recv()

    other_l = (dap, (1 - l) * 2 + c)
    other_core = (dap, l * 2 + 1 - c)
    right_all[right_slot(c, y, l)] = sides[PROJECTED_DIM:]
    right_copy(l, y, right_ls.at[0], other_l).start()

    def to_y(pl_, sems, n):
        return right_copy(pl_, y, sems.at[n], (dap_of(x, zh, y_peer(n)), seq))

    each(1, Y, lambda n: to_y(l, right_ys, n).start())

    def to_core(py, pl_):
        return right_copy(pl_, py, right_cs.at[py * 2 + pl_], other_core)

    to_core(y, l).start()

    left_all[x * ZH + zh] = sides[:PROJECTED_DIM]

    def left_copy(n, slot):
        px, pzh = left_peer(n)
        return copy_to(
            left_all.at[slot], left_all.at[slot], left_ss.at[n], left_rs.at[slot],
            (dap_of(px, pzh, y), seq),
        )

    each(1, LEFTS, lambda n: left_copy(n, x * ZH + zh).start())

    right_arrived(right_slot(c, y, 1 - l))
    each(1, Y, lambda n: to_y(1 - l, right_fs, n).start())
    to_core(y, 1 - l).start()

    att_send[...] = dot_t(ident, attended).astype(BF16).reshape(SEQ, SEQS // SEQ, FEATURES)

    def att_copy(n, slot):
        q = seq_peer(n)
        return copy_to(att_send.at[q], att_ref.at[slot], att_ss.at[n], att_rs.at[slot], (dap, q))

    each(1, SEQ, lambda n: att_copy(n, seq).start())
    att_ref[seq] = att_send[seq]

    def pass_on(pl_, n):
        py = y_peer(n)
        right_arrived(right_slot(c, py, pl_))
        to_core(py, pl_).start()

    each(1, Y, lambda n: pass_on(l, n))
    each(1, Y, lambda n: pass_on(1 - l, n))

    def left_arrived(n):
        px, pzh = left_peer(n)
        left_copy(n, px * ZH + pzh).wait_recv()

    each(1, LEFTS, left_arrived)

    lefts = left_all[...].reshape(LEFTS * PROJECTED_DIM, SEQS).astype(F32)
    left_wide[0] = lefts[:, :128]
    left_wide[1] = lefts[:, 128:]
    each(0, Y * 2, lambda n: right_arrived(right_slot(1 - c, lax.div(n, 2), lax.rem(n, 2))))

    groups = PROJECTED_DIM // 4
    for k in range(4):
        left_k = jnp.concatenate(
            [jnp.concatenate(
                [left_wide[half, pl.ds(4 * g + k, LEFTS, stride=PROJECTED_DIM), :]
                 for half in range(2)], axis=1)
             for g in range(groups)], axis=0).astype(BF16)
        blocks = []
        for py in range(Y):
            for m in range(4):
                j = (m - k) % 4
                blocks.append(right_all[(j % 2) * (Y * 2) + py * 2 + j // 2])
        outer[k] = dot_t(left_k, jnp.concatenate(blocks, axis=0))

    lane_block = lax.broadcasted_iota(jnp.int32, (groups * LEFTS, 128), 1) // PROJECTED_DIM
    for a in range(4):
        flat = []
        for py in range(Y):
            cols = slice(py * 128, (py + 1) * 128)
            chosen = outer[(3 - a) % 4, :, cols]
            for m in range(3):
                chosen = jnp.where(lane_block == m, outer[(m - a) % 4, :, cols], chosen)
            chosen = chosen.astype(BF16)
            flat.append(jnp.concatenate(
                [chosen[g * LEFTS:(g + 1) * LEFTS] for g in range(groups)], axis=1))
        rows_a = jnp.concatenate(
            [couple[(4 * g + (m - a) % 4) * PROJECTED_DIM:(4 * g + (m - a) % 4 + 1) * PROJECTED_DIM, :]
             for g in range(groups) for m in range(4)], axis=0)
        result = dot(jnp.concatenate(flat, axis=0), rows_a)
        for py in range(Y):
            at = (py * 4 + a) * LEFTS
            projected[at:at + LEFTS, :] = result[py * LEFTS:(py + 1) * LEFTS]

    for i in range(LEFTS):
        residue = amino_smem[dap_of(i // ZH, i % ZH, y) * SEQ + seq].astype(F32)
        norm = jnp.maximum(norm_cols[...] * residue, 1.0)
        tiles[i] = (projected[pl.ds(i, RIGHTS, stride=LEFTS), :] / norm).astype(BF16)

    def tile_copy(n):
        px, pzh = left_peer(n)
        return copy_to(
            tiles.at[px * ZH + pzh],
            pair_ref.at[seq, pl.ds(pl.multiple_of(zh * RIGHTS, RIGHTS), RIGHTS)],
            tile_ss.at[n], tile_rs.at[zh * SEQ + seq],
            (dap_of(px, pzh, y), x),
        )

    def own_tile():
        return pltpu.make_async_copy(
            tiles.at[x * ZH + zh],
            pair_ref.at[seq, pl.ds(pl.multiple_of(zh * RIGHTS, RIGHTS), RIGHTS)],
            tile_rs.at[zh * SEQ + seq],
        )

    pl.when(x != seq)(lambda: tile_copy(0).start())
    pl.when(x == seq)(lambda: own_tile().start())
    each(1, LEFTS, lambda n: tile_copy(n).start())

    def tile_arrived(n):
        pzh, pseq = lax.div(n, SEQ), lax.rem(n, SEQ)
        pltpu.make_async_copy(
            tiles.at[0], pair_ref.at[pseq, pl.ds(pl.multiple_of(pzh * RIGHTS, RIGHTS), RIGHTS)],
            tile_rs.at[n],
        ).wait()

    each(0, ZH * SEQ, tile_arrived)
    each(1, SEQ, lambda n: att_copy(n, seq_peer(n)).wait_recv())

    each(1, SEQ, lambda n: stack_copy(n, seq).wait_send())
    each(1, SEQ, lambda n: att_copy(n, seq).wait_send())
    each(1, LEFTS, lambda n: left_copy(n, x * ZH + zh).wait_send())
    right_copy(l, y, right_ls.at[0], other_l).wait_send()
    each(1, Y, lambda n: to_y(l, right_ys, n).wait_send())
    each(1, Y, lambda n: to_y(1 - l, right_fs, n).wait_send())
    each(0, Y * 2, lambda n: to_core(lax.div(n, 2), lax.rem(n, 2)).wait_send())
    pl.when(x != seq)(lambda: tile_copy(0).wait_send())
    each(1, LEFTS, lambda n: tile_copy(n).wait_send())


def on_device(
    homolog_stack,
    homolog_existing_flags,
    amino_existing_flags,
    asking_weights,
    lookup_weights,
    content_weights,
    sigmoid_weights,
    final_projection,
    former_weights,
    latter_weights,
    couple_projection,
):
    block = SEQS // SEQ
    vmem = pl.BlockSpec(memory_space=pltpu.VMEM)
    smem = pl.BlockSpec(memory_space=pltpu.SMEM)
    dma = pltpu.SemaphoreType.DMA
    attended, pair = pl.pallas_call(
        kernel,
        out_shape=(
            jax.ShapeDtypeStruct((SEQ, block, FEATURES), BF16),
            jax.ShapeDtypeStruct((SEQ, ZH * RIGHTS, PAIR), BF16),
        ),
        in_specs=[vmem, vmem, vmem, smem] + [vmem] * 8,
        out_specs=(vmem, vmem),
        scratch_shapes=[
            pltpu.VMEM((SEQ, block, FEATURES), BF16),
            pltpu.VMEM((SEQ, block, FEATURES), BF16),
            pltpu.VMEM((LEFTS, PROJECTED_DIM, SEQS), BF16),
            pltpu.VMEM((RIGHTS, PROJECTED_DIM, SEQS), BF16),
            pltpu.VMEM((4 * FEATURES, FEATURES), BF16),
            pltpu.VMEM((FEATURES, FEATURES), BF16),
            pltpu.VMEM((2 * PROJECTED_DIM, FEATURES), BF16),
            pltpu.VMEM((PROJECTED_DIM * PROJECTED_DIM, PAIR), BF16),
            pltpu.VMEM((SEQS, SEQS), F32),
            pltpu.VMEM((2, LEFTS * PROJECTED_DIM, SEQS // 2), F32),
            pltpu.VMEM((4, PROJECTED_DIM // 4 * LEFTS, RIGHTS * PROJECTED_DIM), F32),
            pltpu.VMEM((RIGHTS * LEFTS, PAIR), F32),
            pltpu.VMEM((LEFTS, RIGHTS, PAIR), BF16),
            pltpu.VMEM((RIGHTS, PAIR), F32),
            dma((SEQ,)), dma((SEQ,)), dma((SEQ,)), dma((SEQ,)),
            dma((LEFTS,)), dma((LEFTS,)),
            dma((1,)), dma((Y,)), dma((Y,)), dma((Y * 2,)), dma((RIGHTS,)),
            dma((LEFTS,)), dma((ZH * SEQ,)),
        ],
        compiler_params=pltpu.CompilerParams(
            collective_id=0, has_side_effects=True, vmem_limit_bytes=40 * 2**20
        ),
        name="column_attention_outer_product",
    )(
        homolog_stack.transpose(1, 0, 2),
        homolog_existing_flags[None, :],
        amino_existing_flags[None, :],
        amino_existing_flags,
        asking_weights, lookup_weights, content_weights, sigmoid_weights, final_projection,
        former_weights.T, latter_weights.T, couple_projection,
    )
    return attended.transpose(1, 0, 2), pair


def solution(mesh):
    in_specs = (P("seq", "dap", None), P(), P(), P(), P(), P(), P(), P(), P(), P(), P())
    out_specs = (P("seq", "dap", None), P("dap", "seq", None))
    return jax.shard_map(
        on_device, mesh=mesh, in_specs=in_specs, out_specs=out_specs, check_vma=False
    )
```

time: 242 us -> 52.4 us (0.22)
  waiting for transfers between devices: 155 us -> 0 us
  Pallas kernels: 0 us -> 43.1 us
  matrix products: 32.4 us -> 0 us
  blocking collectives: 20.5 us -> 0 us
  between operations: 14.4 us -> 0.7 us
  other arithmetic: 8.74 us -> 0 us
    all_gather x1 -> x0, waiting for transfers between devices: 130 us -> none  [on_device(): lax.all_gather(right, 'dap', axis=1, tiled=True)]
    pallas_call x0 -> x1, Pallas kernels: none -> 43.1 us  [on_device(): pl.pallas_call(kernel, out_shape=(jax.ShapeDtypeStruct((SEQ, block, FEATU...]
    dot_general x8 -> x0, matrix products: 31.6 us -> none  [the longest x1 15 us: contract(): jnp.dot(flat_outer, couple_projection, precision=lax.Precision.HIGHEST)]
    reduce_scatter x1 -> x0, waiting for transfers between devices: 25.2 us -> none  [on_device(): lax.psum_scatter(partial_pair, 'seq', scatter_dimension=1, tiled=True)]
    all_gather x2 -> x0, blocking collectives: 20.5 us -> none  [the longest x1 13.2 us: on_device(): lax.all_gather(keys_here, 'seq', axis=0, tiled=True)]
    transpose x2 -> x0, local copies, waits for them, and re-layouts: 9.16 us -> none  [the longest x1 8.24 us: contract(): jnp.einsum('sic,sje->ijce', left_part, right_part, preferred_element_type...]
    unnamed x22 -> x23, local copies, waits for them, and re-layouts: 0.08 us -> 8.24 us
    reduce_sum x5 -> x0, other arithmetic: 3.88 us -> none  [the longest x2 1.39 us: standard_rescale(): variance = jnp.mean(centred * centred, axis=-1, keepdims=True)]
  transfers between devices with their start and end apart: 2 -> 0, of which waited for: 2 -> 0; matrix products, arithmetic and copies ran while one was open for 0% -> 0% of each run, Pallas kernels for 0% -> 0%
where the time goes in v1:
time: 52.4 us; the launch traced here: 52 us
  Pallas kernels  43.1 us (82%)
  local copies, waits for them, and re-layouts  8.24 us (16%)
  between operations  0.7 us (1%)
    pallas_call x1, Pallas kernels, on_device(): pl.pallas_call(kernel, out_shape=(jax.ShapeDtypeStruct((SEQ, block, FEATU...  43.1 us
    unnamed x23, local copies, waits for them, and re-layouts  8.24 us

profile of v1, /device:TPU:1, one launch (start us, length us, event | category | flops | bytes accessed | tf_op | source)
XLA Modules:
  0.0 52.0 jit_solution(16324905356009906011)
XLA Ops:
  0.6 0.0 copy-start.8
  0.6 0.0 copy-start.1
  0.7 0.0 copy-start.2
  0.7 1.0 %copy.16 = bf16[64,4,256]{2,0,1:T(8,128)(2,1)S(1)} copy(bf16[64,4,256]{2,1,0:T(4,128)(2,1)} %param.11) | data formatting | bytes 262144 | tf_op args[0]
  1.6 0.0 copy-start.9
  1.6 0.0 copy-done.8
  1.6 0.0 copy-done.1
  1.7 0.0 copy-done.2
  1.7 0.6 %copy-done.9 = s32[256]{0:T(256)S(1)} copy-done((s32[256]{0:T(256)S(1)}, s32[256]{0:T(256)}, u32[]{:S(2)}) %copy-start.9) | copy-done | bytes 1048
  2.3 0.0 copy-start
  2.3 1.0 %copy-done = f32[1024,128]{1,0:T(8,128)S(1)} copy-done((f32[1024,128]{1,0:T(8,128)S(1)}, f32[1024,128]{1,0:T(8,128)}, u32[]{:S(2)}) %copy-start) | copy-done | bytes 524312
  3.4 0.0 copy-start.3
  3.4 0.9 %copy-done.3 = bf16[256,256]{1,0:T(8,128)(2,1)S(1)} copy-done((bf16[256,256]{1,0:T(8,128)(2,1)S(1)}, bf16[256,256]{1,0:T(8,128)(2,1)}, u32[]{:S(2)}) %copy-start.3) | copy-done | bytes 131096
  4.3 0.0 copy-start.4
  4.3 0.9 %copy-done.4 = bf16[256,256]{1,0:T(8,128)(2,1)S(1)} copy-done((bf16[256,256]{1,0:T(8,128)(2,1)S(1)}, bf16[256,256]{1,0:T(8,128)(2,1)}, u32[]{:S(2)}) %copy-start.4) | copy-done | bytes 131096
  5.2 0.0 copy-start.5
  5.2 0.9 %copy-done.5 = bf16[256,256]{1,0:T(8,128)(2,1)S(1)} copy-done((bf16[256,256]{1,0:T(8,128)(2,1)S(1)}, bf16[256,256]{1,0:T(8,128)(2,1)}, u32[]{:S(2)}) %copy-start.5) | copy-done | bytes 131096
  6.1 0.0 copy-start.6
  6.1 0.7 %copy-done.6 = bf16[256,32]{0,1:T(8,128)(2,1)S(1)} copy-done((bf16[256,32]{0,1:T(8,128)(2,1)S(1)}, bf16[256,32]{0,1:T(8,128)(2,1)}, u32[]{:S(2)}) %copy-start.6) | copy-done | bytes 16408
  6.8 0.0 copy-start.7
  6.8 0.7 %copy-done.7 = bf16[256,32]{0,1:T(8,128)(2,1)S(1)} copy-done((bf16[256,32]{0,1:T(8,128)(2,1)S(1)}, bf16[256,32]{0,1:T(8,128)(2,1)}, u32[]{:S(2)}) %copy-start.7) | copy-done | bytes 16408
  7.5 43.1 %column_attention_outer_product.1 = (bf16[4,64,256]{2,1,0:T(8,128)(2,1)S(1)}, bf16[4,128,128]{2,1,0:T(8,128)(2,1)S(1)}) custom-call(bf16[4,64,256]{2,1,0:T(8,128)(2,1)S(1)} %bitcast.8, s32[1,256]{1,0:T(1,128)S(1)} %bitcast.13, s32[1,512]{1,0:T(1,128)S(1)} %bitcast.12, s32[512]{0:T(512)S(1)} %copy-done.8, bf16[256,256]{1,0:T(8,128)(2,1)S(1)} %copy-done.1, ...), custom_call_target="tpu_custom_call" | custom-call | tf_op jit(solution)/shard_map/column_attention_outer_product/pallas_call | solution.py:332
  50.6 0.8 %copy.14 = bf16[64,4,256]{2,1,0:T(4,128)(2,1)} copy(bf16[64,4,256]{2,0,1:T(8,128)(2,1)S(1)} %bitcast.9) | data formatting | bytes 262144
  51.4 0.7 %copy.18 = bf16[4,128,128]{2,1,0:T(8,128)(2,1)} copy(bf16[4,128,128]{2,1,0:T(8,128)(2,1)S(1)} %get-tuple-element.11) | data formatting | bytes 262144
Async XLA Ops:
  0.6 1.0 %copy-start.8 = (s32[512]{0:T(512)S(1)}, s32[512]{0:T(512)}, u32[]{:S(2)}) copy-start(s32[512]{0:T(512)} %amino_smem.1) | copy-start | bytes 6148
  0.6 1.0 %copy-start.1 = (bf16[256,256]{1,0:T(8,128)(2,1)S(1)}, bf16[256,256]{1,0:T(8,128)(2,1)}, u32[]{:S(2)}) copy-start(bf16[256,256]{1,0:T(8,128)(2,1)} %asking_ref.1) | copy-start | bytes 393220
  0.7 1.0 %copy-start.2 = (bf16[256,256]{1,0:T(8,128)(2,1)S(1)}, bf16[256,256]{1,0:T(8,128)(2,1)}, u32[]{:S(2)}) copy-start(bf16[256,256]{1,0:T(8,128)(2,1)} %lookup_ref.1) | copy-start | bytes 393220
  1.6 0.7 %copy-start.9 = (s32[256]{0:T(256)S(1)}, s32[256]{0:T(256)}, u32[]{:S(2)}) copy-start(s32[256]{0:T(256)} %param.12) | copy-start | bytes 3076
  2.3 1.0 %copy-start = (f32[1024,128]{1,0:T(8,128)S(1)}, f32[1024,128]{1,0:T(8,128)}, u32[]{:S(2)}) copy-start(f32[1024,128]{1,0:T(8,128)} %couple_ref.1) | copy-start | bytes 1572868
  3.4 0.9 %copy-start.3 = (bf16[256,256]{1,0:T(8,128)(2,1)S(1)}, bf16[256,256]{1,0:T(8,128)(2,1)}, u32[]{:S(2)}) copy-start(bf16[256,256]{1,0:T(8,128)(2,1)} %content_ref.1) | copy-start | bytes 393220
  4.3 0.9 %copy-start.4 = (bf16[256,256]{1,0:T(8,128)(2,1)S(1)}, bf16[256,256]{1,0:T(8,128)(2,1)}, u32[]{:S(2)}) copy-start(bf16[256,256]{1,0:T(8,128)(2,1)} %sigmoid_ref.1) | copy-start | bytes 393220
  5.2 0.9 %copy-start.5 = (bf16[256,256]{1,0:T(8,128)(2,1)S(1)}, bf16[256,256]{1,0:T(8,128)(2,1)}, u32[]{:S(2)}) copy-start(bf16[256,256]{1,0:T(8,128)(2,1)} %final_ref.1) | copy-start | bytes 393220
  6.1 0.7 %copy-start.6 = (bf16[256,32]{0,1:T(8,128)(2,1)S(1)}, bf16[256,32]{0,1:T(8,128)(2,1)}, u32[]{:S(2)}) copy-start(bf16[256,32]{0,1:T(8,128)(2,1)} %param.19) | copy-start | bytes 49156
  6.8 0.7 %copy-start.7 = (bf16[256,32]{0,1:T(8,128)(2,1)S(1)}, bf16[256,32]{0,1:T(8,128)(2,1)}, u32[]{:S(2)}) copy-start(bf16[256,32]{0,1:T(8,128)(2,1)} %param.20) | copy-start | bytes 49156

commit v2 on v1

--- a/solution.py
+++ b/solution.py
@@ -14,6 +14,7 @@
 FEATURES = 256
 SEQS = 256
 X, ZH, Y, SEQ = 4, 4, 8, 4
+ROWS_PICKED = 64
 LEFTS = X * ZH
 RIGHTS = Y * SEQ
 MESH = pl.DeviceIdType.MESH
@@ -43,11 +44,13 @@
 
 
 def kernel(
-    stack_ref, homolog_ref, amino_ref, amino_smem,
-    asking_ref, lookup_ref, content_ref, sigmoid_ref, final_ref, former_ref, latter_ref, couple_ref,
+    stack_hbm, homolog_hbm, amino_hbm, asking_hbm, lookup_hbm, content_hbm, sigmoid_hbm, final_hbm,
+    former_hbm, latter_hbm, couple_hbm,
     att_ref, pair_ref,
-    stack_all, att_send, left_all, right_all, wt, wt_final, wt_pair, couple, key_mask,
-    left_wide, outer, projected, tiles, norm_cols,
+    stack_ref, homolog_ref, amino_ref, asking_ref, lookup_ref, content_ref, sigmoid_ref, final_ref,
+    former_ref, latter_ref, couple_ref, local_sems,
+    stack_send, stack_all, att_send, left_all, right_all, wt, wt_final, wt_pair, couple, key_mask,
+    left_wide, outer, projected, tiles, amino_rows,
     stack_ss, stack_rs, att_ss, att_rs, left_ss, left_rs,
     right_ls, right_ys, right_fs, right_cs, right_rs, tile_ss, tile_rs,
 ):
@@ -83,6 +86,18 @@
             return carry
         lax.fori_loop(lo, hi, step, 0)
 
+    local_copies = [
+        pltpu.make_async_copy(src, dst, local_sems.at[n])
+        for n, (src, dst) in enumerate((
+            (stack_hbm, stack_ref), (asking_hbm, asking_ref), (lookup_hbm, lookup_ref),
+            (content_hbm, content_ref), (sigmoid_hbm, sigmoid_ref), (final_hbm, final_ref),
+            (former_hbm, former_ref), (latter_hbm, latter_ref), (homolog_hbm, homolog_ref),
+            (amino_hbm, amino_ref), (couple_hbm, couple_ref),
+        ))
+    ]
+    for copy in local_copies:
+        copy.start()
+
     barrier = pltpu.get_barrier_semaphore()
 
     def greet(device):
@@ -103,6 +118,14 @@
     each(1, ZH * SEQ, greet_tile)
     pl.when(x != seq)(lambda: greet_tile(0))
 
+    rows = lax.broadcasted_iota(jnp.int32, (SEQS, SEQS), 0)
+    cols = lax.broadcasted_iota(jnp.int32, (SEQS, SEQS), 1)
+    block = SEQS // SEQ
+    by_residue = jnp.where(cols == rows % block * SEQ + rows // block, 1.0, 0.0).astype(BF16)
+    for copy in local_copies:
+        copy.wait()
+    stack_send[...] = dot(by_residue, stack_ref[...].reshape(SEQS, FEATURES)).astype(BF16).reshape(
+        SEQ, block, FEATURES)
     ident = eye(FEATURES)
     for n, ref in enumerate((asking_ref, lookup_ref, content_ref, sigmoid_ref)):
         wt[n * FEATURES:(n + 1) * FEATURES, :] = dot_t(ident, ref[...]).astype(BF16)
@@ -115,13 +138,16 @@
     key_mask[...] = dot(diagonal, jnp.ones((SEQS, SEQS), BF16))
     count = jnp.sum(flags, axis=1, keepdims=True)
     residues = amino_ref.shape[1]
-    first_col = dap_of(x, zh, 0) * SEQ
-    rows = lax.broadcasted_iota(jnp.int32, (RIGHTS, residues), 0)
-    cols = lax.broadcasted_iota(jnp.int32, (RIGHTS, residues), 1)
-    picked = jnp.where(cols == rows + first_col, 1.0, 0.0).astype(BF16)
+    shape = (ROWS_PICKED, residues)
+    rows = lax.broadcasted_iota(jnp.int32, shape, 0)
+    cols = lax.broadcasted_iota(jnp.int32, shape, 1)
+    wanted = jnp.where(
+        rows < RIGHTS, rows + dap_of(x, zh, 0) * SEQ,
+        jnp.where(rows < RIGHTS + LEFTS, (rows - RIGHTS) * RIGHTS + y * SEQ + seq, dap * SEQ + seq),
+    )
+    picked = jnp.where(cols == wanted, 1.0, 0.0).astype(BF16)
     amino_wide = jnp.broadcast_to(amino_ref[...].astype(F32), (PAIR, residues)).astype(BF16)
-    norm_cols[...] = dot_t(picked, amino_wide) * count
-    amino_here = amino_smem[dap * SEQ + seq].astype(F32)
+    amino_rows[...] = dot_t(picked, amino_wide)
 
     greeted = SEQ - 1 + LEFTS - 1 + Y - 1 + ZH * SEQ
     pl.when(x != seq)(lambda: pl.semaphore_wait(barrier, greeted))
@@ -129,10 +155,10 @@
 
     def stack_copy(n, slot):
         q = seq_peer(n)
-        return copy_to(stack_ref.at[q], stack_all.at[slot], stack_ss.at[n], stack_rs.at[slot], (dap, q))
+        return copy_to(stack_send.at[q], stack_all.at[slot], stack_ss.at[n], stack_rs.at[slot], (dap, q))
 
     each(1, SEQ, lambda n: stack_copy(n, seq).start())
-    stack_all[seq] = stack_ref[seq]
+    stack_all[seq] = stack_send[seq]
     each(1, SEQ, lambda n: stack_copy(n, seq_peer(n)).wait_recv())
 
     incoming = dot_t(ident, stack_all[...].reshape(SEQS, FEATURES))
@@ -162,8 +188,9 @@
     gated = jnp.concatenate(gated, axis=0)
     attended = (incoming + dot(wt_final[...], gated)).astype(BF16)
 
+    amino_here = amino_rows[RIGHTS + LEFTS:RIGHTS + LEFTS + 1, :]
     normed2 = rescale_rows(attended.astype(F32)).astype(BF16)
-    sides = (dot(wt_pair[...], normed2) * (flags * amino_here)).astype(BF16)
+    sides = (dot(wt_pair[...], normed2) * (flags * jnp.concatenate([amino_here, amino_here], axis=1))).astype(BF16)
 
     def right_slot(core, py, pl_):
         return core * (Y * 2) + py * 2 + pl_
@@ -266,9 +293,9 @@
             at = (py * 4 + a) * LEFTS
             projected[at:at + LEFTS, :] = result[py * LEFTS:(py + 1) * LEFTS]
 
+    norm_cols = amino_rows[:RIGHTS, :] * count
     for i in range(LEFTS):
-        residue = amino_smem[dap_of(i // ZH, i % ZH, y) * SEQ + seq].astype(F32)
-        norm = jnp.maximum(norm_cols[...] * residue, 1.0)
+        norm = jnp.maximum(norm_cols * amino_rows[RIGHTS + i:RIGHTS + i + 1, :], 1.0)
         tiles[i] = (projected[pl.ds(i, RIGHTS, stride=LEFTS), :] / norm).astype(BF16)
 
     def tile_copy(n):
@@ -327,17 +354,26 @@
 ):
     block = SEQS // SEQ
     vmem = pl.BlockSpec(memory_space=pltpu.VMEM)
-    smem = pl.BlockSpec(memory_space=pltpu.SMEM)
+    hbm = pl.BlockSpec(memory_space=pltpu.HBM)
     dma = pltpu.SemaphoreType.DMA
+    operands = (
+        homolog_stack,
+        homolog_existing_flags[None, :],
+        amino_existing_flags[None, :],
+        asking_weights, lookup_weights, content_weights, sigmoid_weights, final_projection,
+        former_weights.T, latter_weights.T, couple_projection,
+    )
     attended, pair = pl.pallas_call(
         kernel,
         out_shape=(
-            jax.ShapeDtypeStruct((SEQ, block, FEATURES), BF16),
-            jax.ShapeDtypeStruct((SEQ, ZH * RIGHTS, PAIR), BF16),
+            pltpu.VMEM((SEQ, block, FEATURES), BF16),
+            pltpu.VMEM((SEQ, ZH * RIGHTS, PAIR), BF16),
         ),
-        in_specs=[vmem, vmem, vmem, smem] + [vmem] * 8,
+        in_specs=[hbm] * len(operands),
         out_specs=(vmem, vmem),
-        scratch_shapes=[
+        scratch_shapes=[pltpu.VMEM(a.shape, a.dtype) for a in operands] + [
+            dma((len(operands),)),
+            pltpu.VMEM((SEQ, block, FEATURES), BF16),
             pltpu.VMEM((SEQ, block, FEATURES), BF16),
             pltpu.VMEM((SEQ, block, FEATURES), BF16),
             pltpu.VMEM((LEFTS, PROJECTED_DIM, SEQS), BF16),
@@ -351,24 +387,17 @@
             pltpu.VMEM((4, PROJECTED_DIM // 4 * LEFTS, RIGHTS * PROJECTED_DIM), F32),
             pltpu.VMEM((RIGHTS * LEFTS, PAIR), F32),
             pltpu.VMEM((LEFTS, RIGHTS, PAIR), BF16),
-            pltpu.VMEM((RIGHTS, PAIR), F32),
+            pltpu.VMEM((ROWS_PICKED, PAIR), F32),
             dma((SEQ,)), dma((SEQ,)), dma((SEQ,)), dma((SEQ,)),
             dma((LEFTS,)), dma((LEFTS,)),
             dma((1,)), dma((Y,)), dma((Y,)), dma((Y * 2,)), dma((RIGHTS,)),
             dma((LEFTS,)), dma((ZH * SEQ,)),
         ],
         compiler_params=pltpu.CompilerParams(
-            collective_id=0, has_side_effects=True, vmem_limit_bytes=40 * 2**20
+            collective_id=0, has_side_effects=True, vmem_limit_bytes=60 * 2**20
         ),
         name="column_attention_outer_product",
-    )(
-        homolog_stack.transpose(1, 0, 2),
-        homolog_existing_flags[None, :],
-        amino_existing_flags[None, :],
-        amino_existing_flags,
-        asking_weights, lookup_weights, content_weights, sigmoid_weights, final_projection,
-        former_weights.T, latter_weights.T, couple_projection,
-    )
+    )(*operands)
     return attended.transpose(1, 0, 2), pair
 
 

time: 52.4 us -> 45 us (0.86)
  local copies, waits for them, and re-layouts: 8.24 us -> 1.41 us
    unnamed x23 -> x2, local copies, waits for them, and re-layouts: 8.24 us -> 1.41 us
where the time goes in v2:
time: 45 us; the launch traced here: 44.9 us
  Pallas kernels  42.8 us (95%)
  local copies, waits for them, and re-layouts  1.41 us (3%)
  between operations  0.64 us (1%)
    pallas_call x1, Pallas kernels, on_device(): pl.pallas_call(kernel, out_shape=(pltpu.VMEM((SEQ, block, FEATURES), BF16...  42.8 us
    unnamed x2, local copies, waits for them, and re-layouts  1.41 us

profile of v2, /device:TPU:1, one launch (start us, length us, event | category | flops | bytes accessed | tf_op | source)
XLA Modules:
  0.0 44.9 jit_solution(3566463272697497260)
XLA Ops:
  0.6 42.8 %column_attention_outer_product.1 = (bf16[4,64,256]{2,1,0:T(8,128)(2,1)S(1)}, bf16[4,128,128]{2,1,0:T(8,128)(2,1)S(1)}) custom-call(bf16[64,4,256]{2,1,0:T(4,128)(2,1)} %stack_hbm.1, s32[1,256]{1,0:T(1,128)} %bitcast.9, s32[1,512]{1,0:T(1,128)} %bitcast.8, bf16[256,256]{1,0:T(8,128)(2,1)} %asking_hbm.1, bf16[256,256]{1,0:T(8,128)(2,1)} %lookup_hbm.1, ...), custom_call_target="tpu_custom_call" | custom-call | tf_op jit(solution)/shard_map/column_attention_outer_product/pallas_call | solution.py:366
  43.5 0.8 %copy.13 = bf16[64,4,256]{2,1,0:T(4,128)(2,1)} copy(bf16[64,4,256]{2,0,1:T(8,128)(2,1)S(1)} %bitcast.5) | data formatting | bytes 262144
  44.2 0.7 %copy.15 = bf16[4,128,128]{2,1,0:T(8,128)(2,1)} copy(bf16[4,128,128]{2,1,0:T(8,128)(2,1)S(1)} %get-tuple-element.9) | data formatting | bytes 262144

commit v3 on v2

--- a/solution.py
+++ b/solution.py
@@ -51,7 +51,7 @@
     former_ref, latter_ref, couple_ref, local_sems,
     stack_send, stack_all, att_send, left_all, right_all, wt, wt_final, wt_pair, couple, key_mask,
     left_wide, outer, projected, tiles, amino_rows,
-    stack_ss, stack_rs, att_ss, att_rs, left_ss, left_rs,
+    here_sems, stack_ss, stack_rs, att_ss, att_rs, left_ss, left_rs,
     right_ls, right_ys, right_fs, right_cs, right_rs, tile_ss, tile_rs,
 ):
     dap = lax.axis_index("dap")
@@ -103,29 +103,54 @@
     def greet(device):
         pl.semaphore_signal(barrier, inc=1, device_id=device, device_id_type=MESH)
 
+    def along_x(n):
+        return lax.rem(x + n, X)
+
     each(1, SEQ, lambda n: greet((dap, seq_peer(n))))
-
-    def greet_left(n):
-        px, pzh = left_peer(n)
+    each(1, X, lambda n: greet((dap_of(along_x(n), zh, y), seq)))
+    each(1, Y, lambda n: greet((dap_of(x, zh, y_peer(n)), seq)))
+    above = (ZH - 1 - zh) * X
+    below = zh * X
+
+    def peer_above(n):
+        return along_x(lax.rem(n, X)), zh + 1 + lax.div(n, X)
+
+    def peer_below(n):
+        return along_x(lax.rem(n, X)), zh - 1 - lax.div(n, X)
+
+    def greet_above(n):
+        px, pzh = peer_above(n)
         greet((dap_of(px, pzh, y), seq))
 
-    each(1, LEFTS, greet_left)
-    each(1, Y, lambda n: greet((dap_of(x, zh, y_peer(n)), seq)))
-
-    def greet_tile(n):
-        greet((dap_of(seq, lax.rem(zh + lax.div(n, SEQ), ZH), y), lax.rem(seq + lax.rem(n, SEQ), SEQ)))
-
-    each(1, ZH * SEQ, greet_tile)
-    pl.when(x != seq)(lambda: greet_tile(0))
+    each(0, above, greet_above)
 
     rows = lax.broadcasted_iota(jnp.int32, (SEQS, SEQS), 0)
     cols = lax.broadcasted_iota(jnp.int32, (SEQS, SEQS), 1)
     block = SEQS // SEQ
     by_residue = jnp.where(cols == rows % block * SEQ + rows // block, 1.0, 0.0).astype(BF16)
-    for copy in local_copies:
-        copy.wait()
+    local_copies[0].wait()
     stack_send[...] = dot(by_residue, stack_ref[...].reshape(SEQS, FEATURES)).astype(BF16).reshape(
         SEQ, block, FEATURES)
+
+    pl.semaphore_wait(barrier, SEQ - 1 + X - 1 + Y - 1 + below)
+
+    def answer(n):
+        px, pzh = peer_below(n)
+        pl.semaphore_signal(
+            here_sems.at[x * ZH + zh], inc=1, device_id=(dap_of(px, pzh, y), seq), device_id_type=MESH
+        )
+
+    each(0, below, answer)
+
+    def stack_copy(n, slot):
+        q = seq_peer(n)
+        return copy_to(stack_send.at[q], stack_all.at[slot], stack_ss.at[n], stack_rs.at[slot], (dap, q))
+
+    each(1, SEQ, lambda n: stack_copy(n, seq).start())
+    stack_all[seq] = stack_send[seq]
+
+    for copy in local_copies[1:]:
+        copy.wait()
     ident = eye(FEATURES)
     for n, ref in enumerate((asking_ref, lookup_ref, content_ref, sigmoid_ref)):
         wt[n * FEATURES:(n + 1) * FEATURES, :] = dot_t(ident, ref[...]).astype(BF16)
@@ -149,16 +174,6 @@
     amino_wide = jnp.broadcast_to(amino_ref[...].astype(F32), (PAIR, residues)).astype(BF16)
     amino_rows[...] = dot_t(picked, amino_wide)
 
-    greeted = SEQ - 1 + LEFTS - 1 + Y - 1 + ZH * SEQ
-    pl.when(x != seq)(lambda: pl.semaphore_wait(barrier, greeted))
-    pl.when(x == seq)(lambda: pl.semaphore_wait(barrier, greeted - 1))
-
-    def stack_copy(n, slot):
-        q = seq_peer(n)
-        return copy_to(stack_send.at[q], stack_all.at[slot], stack_ss.at[n], stack_rs.at[slot], (dap, q))
-
-    each(1, SEQ, lambda n: stack_copy(n, seq).start())
-    stack_all[seq] = stack_send[seq]
     each(1, SEQ, lambda n: stack_copy(n, seq_peer(n)).wait_recv())
 
     incoming = dot_t(ident, stack_all[...].reshape(SEQS, FEATURES))
@@ -219,18 +234,29 @@
 
     left_all[x * ZH + zh] = sides[:PROJECTED_DIM]
 
-    def left_copy(n, slot):
-        px, pzh = left_peer(n)
+    def left_copy(px, pzh, slot):
+        there = px * ZH + pzh
         return copy_to(
-            left_all.at[slot], left_all.at[slot], left_ss.at[n], left_rs.at[slot],
+            left_all.at[slot], left_all.at[slot], left_ss.at[there], left_rs.at[slot],
             (dap_of(px, pzh, y), seq),
         )
 
-    each(1, LEFTS, lambda n: left_copy(n, x * ZH + zh).start())
+    def left_send(px, pzh):
+        left_copy(px, pzh, x * ZH + zh).start()
+
+    each(0, below, lambda n: left_send(*peer_below(n)))
+    each(1, X, lambda n: left_send(along_x(n), zh))
 
     right_arrived(right_slot(c, y, 1 - l))
     each(1, Y, lambda n: to_y(1 - l, right_fs, n).start())
     to_core(y, 1 - l).start()
+
+    def left_send_above(n):
+        px, pzh = peer_above(n)
+        pl.semaphore_wait(here_sems.at[px * ZH + pzh], 1)
+        left_send(px, pzh)
+
+    each(0, above, left_send_above)
 
     att_send[...] = dot_t(ident, attended).astype(BF16).reshape(SEQ, SEQS // SEQ, FEATURES)
 
@@ -251,7 +277,7 @@
 
     def left_arrived(n):
         px, pzh = left_peer(n)
-        left_copy(n, px * ZH + pzh).wait_recv()
+        left_copy(px, pzh, px * ZH + pzh).wait_recv()
 
     each(1, LEFTS, left_arrived)
 
@@ -330,7 +356,12 @@
 
     each(1, SEQ, lambda n: stack_copy(n, seq).wait_send())
     each(1, SEQ, lambda n: att_copy(n, seq).wait_send())
-    each(1, LEFTS, lambda n: left_copy(n, x * ZH + zh).wait_send())
+
+    def left_gone(n):
+        px, pzh = left_peer(n)
+        left_copy(px, pzh, x * ZH + zh).wait_send()
+
+    each(1, LEFTS, left_gone)
     right_copy(l, y, right_ls.at[0], other_l).wait_send()
     each(1, Y, lambda n: to_y(l, right_ys, n).wait_send())
     each(1, Y, lambda n: to_y(1 - l, right_fs, n).wait_send())
@@ -388,6 +419,7 @@
             pltpu.VMEM((RIGHTS * LEFTS, PAIR), F32),
             pltpu.VMEM((LEFTS, RIGHTS, PAIR), BF16),
             pltpu.VMEM((ROWS_PICKED, PAIR), F32),
+            pltpu.SemaphoreType.REGULAR((LEFTS,)),
             dma((SEQ,)), dma((SEQ,)), dma((SEQ,)), dma((SEQ,)),
             dma((LEFTS,)), dma((LEFTS,)),
             dma((1,)), dma((Y,)), dma((Y,)), dma((Y * 2,)), dma((RIGHTS,)),

time: 45 us -> 43.5 us (0.967)
  Pallas kernels: 42.8 us -> 41.3 us
    pallas_call x1, Pallas kernels: 42.8 us -> 41.3 us  [on_device(): pl.pallas_call(kernel, out_shape=(pltpu.VMEM((SEQ, block, FEATURES), BF16...]
where the time goes in v3:
time: 43.5 us; the launch traced here: 43.4 us
  Pallas kernels  41.3 us (95%)
  local copies, waits for them, and re-layouts  1.41 us (3%)
  between operations  0.64 us (1%)
    pallas_call x1, Pallas kernels, on_device(): pl.pallas_call(kernel, out_shape=(pltpu.VMEM((SEQ, block, FEATURES), BF16...  41.3 us
    unnamed x2, local copies, waits for them, and re-layouts  1.41 us

profile of v3, /device:TPU:1, one launch (start us, length us, event | category | flops | bytes accessed | tf_op | source)
XLA Modules:
  0.0 43.4 jit_solution(3919608116418359429)
XLA Ops:
  0.6 41.3 %column_attention_outer_product.1 = (bf16[4,64,256]{2,1,0:T(8,128)(2,1)S(1)}, bf16[4,128,128]{2,1,0:T(8,128)(2,1)S(1)}) custom-call(bf16[64,4,256]{2,1,0:T(4,128)(2,1)} %stack_hbm.1, s32[1,256]{1,0:T(1,128)} %bitcast.9, s32[1,512]{1,0:T(1,128)} %bitcast.8, bf16[256,256]{1,0:T(8,128)(2,1)} %asking_hbm.1, bf16[256,256]{1,0:T(8,128)(2,1)} %lookup_hbm.1, ...), custom_call_target="tpu_custom_call" | custom-call | tf_op jit(solution)/shard_map/column_attention_outer_product/pallas_call | solution.py:397
  41.9 0.8 %copy.13 = bf16[64,4,256]{2,1,0:T(4,128)(2,1)} copy(bf16[64,4,256]{2,0,1:T(8,128)(2,1)S(1)} %bitcast.5) | data formatting | bytes 262144
  42.7 0.7 %copy.15 = bf16[4,128,128]{2,1,0:T(8,128)(2,1)} copy(bf16[4,128,128]{2,1,0:T(8,128)(2,1)S(1)} %get-tuple-element.9) | data formatting | bytes 262144

commit v4 on v2

v4 whole, which is shorter than its diff:
```python
import functools

import jax
import jax.numpy as jnp
from jax import lax
from jax.experimental import pallas as pl
from jax.experimental.pallas import tpu as pltpu
from jax.sharding import PartitionSpec as P

HEADS = 8
PER_HEAD_DIM = 32
PROJECTED_DIM = 32
PAIR = 128
FEATURES = 256
SEQS = 256
X, ZH, Y, SEQ = 4, 4, 8, 4
ROWS_PICKED = 64
LEFTS = X * ZH * 2
RIGHTS = Y * 2
PLANE = X * 2
TILES = X * ZH
MESH = pl.DeviceIdType.MESH
F32 = jnp.float32
BF16 = jnp.bfloat16


def dot(a, b):
    return lax.dot_general(a, b, (((1,), (0,)), ((), ())), preferred_element_type=F32)


def dot_t(a, b):
    return lax.dot_general(a, b, (((1,), (1,)), ((), ())), preferred_element_type=F32)


def eye(size):
    rows = lax.broadcasted_iota(jnp.int32, (size, size), 0)
    cols = lax.broadcasted_iota(jnp.int32, (size, size), 1)
    return jnp.where(rows == cols, 1.0, 0.0).astype(BF16)


def rescale_rows(values):
    mean = jnp.mean(values, axis=0, keepdims=True)
    centred = values - mean
    variance = jnp.mean(centred * centred, axis=0, keepdims=True)
    return centred * lax.rsqrt(variance + 1e-05)


def kernel(
    stack_hbm, homolog_hbm, amino_hbm, asking_hbm, lookup_hbm, content_hbm, sigmoid_hbm, final_hbm,
    former_hbm, latter_hbm, couple_hbm,
    att_ref, pair_ref,
    stack_ref, homolog_ref, amino_ref, asking_ref, lookup_ref, content_ref, sigmoid_ref, final_ref,
    former_ref, latter_ref, couple_ref, local_sems,
    stack_send, stack_all, att_send, left_all, right_all, wt, wt_final, wt_pair, couple, key_mask,
    left_wide, outer, projected, tiles, tiles_in, pair_wide, amino_rows,
    here_sems, stack_ss, stack_rs, att_ss, att_rs, left_ss, left_rs,
    right_ss, right_rs, tile_ss, tile_rs,
):
    dap = lax.axis_index("dap")
    seq = lax.axis_index("seq")
    x, zh, y = lax.div(dap, ZH * Y), lax.rem(lax.div(dap, Y), ZH), lax.rem(dap, Y)
    l, c = lax.div(seq, 2), lax.rem(seq, 2)

    def dap_of(px, pzh, py):
        return (px * ZH + pzh) * Y + py

    xs = [x] + [lax.rem(x + n, X) for n in range(1, X)]
    zs = [zh] + [lax.rem(zh + n, ZH) for n in range(1, ZH)]
    ys = [y] + [lax.rem(y + n, Y) for n in range(1, Y)]
    qs = [seq] + [lax.rem(seq + n, SEQ) for n in range(1, SEQ)]

    def copy_to(src, dst, send_sem, recv_sem, device):
        return pltpu.make_async_remote_copy(
            src_ref=src, dst_ref=dst, send_sem=send_sem, recv_sem=recv_sem,
            device_id=device, device_id_type=MESH,
        )

    def each(lo, hi, body):
        def step(n, carry):
            body(n)
            return carry
        lax.fori_loop(lo, hi, step, 0)

    local_copies = [
        pltpu.make_async_copy(src, dst, local_sems.at[n])
        for n, (src, dst) in enumerate((
            (stack_hbm, stack_ref), (asking_hbm, asking_ref), (lookup_hbm, lookup_ref),
            (content_hbm, content_ref), (sigmoid_hbm, sigmoid_ref), (final_hbm, final_ref),
            (former_hbm, former_ref), (latter_hbm, latter_ref), (homolog_hbm, homolog_ref),
            (amino_hbm, amino_ref), (couple_hbm, couple_ref),
        ))
    ]
    local_copies[0].start()

    barrier = pltpu.get_barrier_semaphore()

    def greet(device):
        pl.semaphore_signal(barrier, inc=1, device_id=device, device_id_type=MESH)

    for q in qs[1:]:
        greet((dap, q))
    for py in ys[1:]:
        greet((dap_of(x, zh, py), seq))
    for px in xs[1:]:
        greet((dap_of(px, zh, y), seq))
    each(zh + 1, ZH, lambda pzh: greet((dap_of(x, pzh, y), seq)))
    for copy in local_copies[1:]:
        copy.start()

    rows = lax.broadcasted_iota(jnp.int32, (SEQS, SEQS), 0)
    cols = lax.broadcasted_iota(jnp.int32, (SEQS, SEQS), 1)
    block = SEQS // SEQ
    by_residue = jnp.where(cols == rows % block * SEQ + rows // block, 1.0, 0.0).astype(BF16)
    local_copies[0].wait()
    stack_send[...] = dot(by_residue, stack_ref[...].reshape(SEQS, FEATURES)).astype(BF16).reshape(
        SEQ, block, FEATURES)

    pl.semaphore_wait(barrier, SEQ - 1 + X - 1 + Y - 1 + zh)

    def stack_copy(n, slot):
        return copy_to(
            stack_send.at[qs[n]], stack_all.at[slot], stack_ss.at[n], stack_rs.at[slot], (dap, qs[n]))

    for n in range(1, SEQ):
        stack_copy(n, seq).start()

    def answer(pzh):
        pl.semaphore_signal(
            here_sems.at[zh], inc=1, device_id=(dap_of(x, pzh, y), seq), device_id_type=MESH)

    each(0, zh, answer)
    stack_all[seq] = stack_send[seq]

    for copy in local_copies[1:]:
        copy.wait()
    ident = eye(FEATURES)
    for n, ref in enumerate((asking_ref, lookup_ref, content_ref, sigmoid_ref)):
        wt[n * FEATURES:(n + 1) * FEATURES, :] = dot_t(ident, ref[...]).astype(BF16)
    wt_final[...] = dot_t(ident, final_ref[...]).astype(BF16)
    wt_pair[:PROJECTED_DIM, :] = former_ref[...]
    wt_pair[PROJECTED_DIM:, :] = latter_ref[...]
    couple[...] = couple_ref[...].astype(BF16)
    flags = homolog_ref[...].astype(F32)
    diagonal = (ident.astype(F32) * flags).astype(BF16)
    key_mask[...] = dot(diagonal, jnp.ones((SEQS, SEQS), BF16))
    count = jnp.sum(flags, axis=1, keepdims=True)
    residues = amino_ref.shape[1]
    shape = (ROWS_PICKED, residues)
    rows = lax.broadcasted_iota(jnp.int32, shape, 0)
    cols = lax.broadcasted_iota(jnp.int32, shape, 1)
    wanted = jnp.where(
        rows < RIGHTS, dap_of(x, zh, 0) * SEQ + 2 * rows + c,
        jnp.where(
            rows < RIGHTS + LEFTS,
            dap_of((rows - RIGHTS) % X, (rows - RIGHTS) // PLANE, y) * SEQ + 2 * l
            + (rows - RIGHTS) // X % 2,
            dap * SEQ + seq,
        ),
    )
    picked = jnp.where(cols == wanted, 1.0, 0.0).astype(BF16)
    amino_wide = jnp.broadcast_to(amino_ref[...].astype(F32), (PAIR, residues)).astype(BF16)
    amino_rows[...] = dot_t(picked, amino_wide)

    for n in range(1, SEQ):
        stack_copy(n, qs[n]).wait_recv()

    incoming = dot_t(ident, stack_all[...].reshape(SEQS, FEATURES))
    normed = rescale_rows(incoming).astype(BF16)
    query = (dot(wt[0:256, :], normed) * PER_HEAD_DIM ** (-0.5)).astype(BF16)
    key_t = dot(wt[256:512, :], normed).astype(BF16)
    value = dot(wt[512:768, :], normed).astype(BF16)
    gate = jax.nn.sigmoid(dot(wt[768:1024, :], normed))
    key = dot_t(ident, key_t).astype(BF16)
    here = key_mask[...] > 0.5
    gated = []
    for h in range(HEADS):
        lo = h * PER_HEAD_DIM
        group = lo // 128 * 128
        before, after = lo - group, 128 - PER_HEAD_DIM - (lo - group)
        parts = [query[lo:lo + PER_HEAD_DIM]]
        if before:
            parts.insert(0, jnp.zeros((before, SEQS), BF16))
        if after:
            parts.append(jnp.zeros((after, SEQS), BF16))
        scores = dot(key[:, group:group + 128], jnp.concatenate(parts, axis=0))
        scores = jnp.where(here, scores, -1000000000.0)
        weights = jnp.exp(scores - jnp.max(scores, axis=0, keepdims=True))
        total = jnp.sum(weights, axis=0, keepdims=True)
        mixed = dot(value[lo:lo + PER_HEAD_DIM], weights.astype(BF16))
        gated.append((gate[lo:lo + PER_HEAD_DIM] * (mixed / total)).astype(BF16))
    gated = jnp.concatenate(gated, axis=0)
    attended = (incoming + dot(wt_final[...], gated)).astype(BF16)

    amino_here = amino_rows[RIGHTS + LEFTS:RIGHTS + LEFTS + 1, :]
    normed2 = rescale_rows(attended.astype(F32)).astype(BF16)
    sides = (dot(wt_pair[...], normed2) * (flags * jnp.concatenate([amino_here, amino_here], axis=1))).astype(BF16)

    def right_copy(slot, send_sem, device):
        ref = right_all.at[slot]
        return copy_to(ref, ref, send_sem, right_rs.at[slot], device)

    def right_arrived(slot):
        right_copy(slot, right_ss.at[0], (dap, qs[1])).wait_recv()

    other_l = (dap, (1 - l) * 2 + c)
    other_core = (dap, l * 2 + 1 - c)
    right_sent = []

    def send_right(slot, device):
        copy = right_copy(slot, right_ss.at[len(right_sent)], device)
        copy.start()
        right_sent.append(copy)

    own = y * 2 + l

    def left_slot(core, px, pzh):
        return pzh * PLANE + core * X + px

    def left_copy(px, pzh, n, device):
        slot = left_slot(c, px, pzh)
        return copy_to(left_all.at[slot], left_all.at[slot], left_ss.at[n], left_rs.at[slot], device)

    def along_z(pzh):
        return left_copy(x, zh, pzh, (dap_of(x, pzh, y), seq))

    def along_x(pzh, n):
        return left_copy(x, pzh, ZH + pzh * X + n, (dap_of(xs[n], zh, y), seq))

    def to_core(px, pzh):
        return left_copy(px, pzh, ZH + TILES + px * ZH + pzh, other_core)

    def spread(pzh):
        for n in (1, 3, 2):
            along_x(pzh, n).start()
        to_core(x, pzh).start()

    def left_arrived(px, pzh):
        left_copy(px, pzh, 0, (dap, qs[1])).wait_recv()

    def pass_left(pzh):
        left_arrived(x, pzh)
        spread(pzh)

    def take_left(pzh):
        for n in (1, 3, 2):
            left_arrived(xs[n], pzh)
            to_core(xs[n], pzh).start()

    left_all[left_slot(c, x, zh)] = sides[:PROJECTED_DIM]
    each(0, zh, lambda pzh: along_z(pzh).start())
    right_all[own] = sides[PROJECTED_DIM:]
    send_right(own, other_l)
    for n in (1, 7, 2, 6, 3, 5, 4):
        send_right(own, (dap_of(x, zh, ys[n]), seq))
    spread(zh)

    def send_above(pzh):
        pl.semaphore_wait(here_sems.at[pzh], 1)
        along_z(pzh).start()

    each(zh + 1, ZH, send_above)

    def pass_y(n):
        slot = ys[n] * 2 + l
        right_arrived(slot)
        send_right(slot, other_l)

    att_send[...] = dot_t(ident, attended).astype(BF16).reshape(SEQ, SEQS // SEQ, FEATURES)
    pass_y(1)
    pass_y(7)
    each(0, zh, pass_left)
    pass_y(2)
    pass_y(6)
    pass_y(3)
    pass_y(5)
    pass_y(4)
    each(0, zh + 1, take_left)

    def att_copy(n, slot):
        return copy_to(
            att_send.at[qs[n]], att_ref.at[slot], att_ss.at[n], att_rs.at[slot], (dap, qs[n]))

    for n in range(1, SEQ):
        att_copy(n, seq).start()
    att_ref[seq] = att_send[seq]

    each(zh + 1, ZH, pass_left)
    for py in range(Y):
        right_arrived(py * 2 + 1 - l)

    def left_of_core(px, pzh):
        slot = left_slot(1 - c, px, pzh)
        ref = left_all.at[slot]
        copy_to(ref, ref, left_ss.at[0], left_rs.at[slot], other_core).wait_recv()

    def tile_copy(plane, n):
        return copy_to(
            tiles.at[plane * X + xs[n]], tiles_in.at[zh * SEQ + seq],
            tile_ss.at[plane * X + n], tile_rs.at[zh * SEQ + seq],
            (dap_of(xs[n], plane, y), x),
        )

    def is_own(plane):
        return jnp.logical_and(x == seq, zh == plane)

    def own_tile(plane):
        return pltpu.make_async_copy(
            tiles.at[plane * X + x], tiles_in.at[zh * SEQ + seq], tile_rs.at[zh * SEQ + seq])

    groups = PROJECTED_DIM // 4
    turns = RIGHTS // 4
    lane_block = lax.broadcasted_iota(jnp.int32, (groups * PLANE, 128), 1) // PROJECTED_DIM
    norm_cols = amino_rows[:RIGHTS, :] * count

    def multiply(plane):
        first = plane * PLANE
        lefts = left_all[first:first + PLANE].reshape(PLANE * PROJECTED_DIM, SEQS).astype(F32)
        for half in range(2):
            left_wide[plane, half] = lefts[:, half * 128:(half + 1) * 128]
        for k in range(4):
            left_k = jnp.concatenate(
                [jnp.concatenate(
                    [left_wide[plane, half, pl.ds(4 * g + k, PLANE, stride=PROJECTED_DIM), :]
                     for half in range(2)], axis=1)
                 for g in range(groups)], axis=0).astype(BF16)
            blocks = [right_all[4 * turn + (m - k) % 4] for turn in range(turns) for m in range(4)]
            outer[plane, k] = dot_t(left_k, jnp.concatenate(blocks, axis=0))
        for a in range(4):
            flat = []
            for turn in range(turns):
                cols = slice(turn * 128, (turn + 1) * 128)
                chosen = outer[plane, (3 - a) % 4, :, cols]
                for m in range(3):
                    chosen = jnp.where(lane_block == m, outer[plane, (m - a) % 4, :, cols], chosen)
                flat.append(jnp.concatenate(
                    [chosen[g * PLANE:(g + 1) * PLANE] for g in range(groups)], axis=1))
            rows_a = jnp.concatenate(
                [couple[(4 * g + (m - a) % 4) * PROJECTED_DIM:(4 * g + (m - a) % 4 + 1) * PROJECTED_DIM, :]
                 for g in range(groups) for m in range(4)], axis=0)
            result = dot(jnp.concatenate(flat, axis=0).astype(BF16), rows_a)
            for turn in range(turns):
                at = (turn * 4 + a) * PLANE
                projected[plane, at:at + PLANE, :] = result[turn * PLANE:(turn + 1) * PLANE]
        for n in range(PLANE):
            i = RIGHTS + first + n
            norm = jnp.maximum(norm_cols * amino_rows[i:i + 1, :], 1.0)
            tiles[plane * X + n % X, n // X] = (
                projected[plane, pl.ds(n, RIGHTS, stride=PLANE), :] / norm).astype(BF16)

    for plane in range(ZH):
        pl.when(zh < plane)(functools.partial(take_left, plane))
        for px in range(X):
            left_of_core(px, plane)
        multiply(plane)
        for n in (1, 3, 2):
            tile_copy(plane, n).start()
        pl.when(jnp.logical_not(is_own(plane)))(lambda: tile_copy(plane, 0).start())
        pl.when(is_own(plane))(lambda: own_tile(plane).start())

    for n in range(1, SEQ):
        att_copy(n, qs[n]).wait_recv()

    for pzh in range(ZH):
        for pseq in range(SEQ):
            slot = pzh * SEQ + pseq
            pltpu.make_async_copy(tiles.at[0], tiles_in.at[slot], tile_rs.at[slot]).wait()
            for row in range(2):
                at = (pseq // 2 * 2 + row) * TILES * 8 + pzh * RIGHTS * 2 + pseq % 2
                pair_wide[pl.ds(at, RIGHTS, stride=2), :] = tiles_in[slot, row].astype(F32)
    pair_ref[...] = pair_wide[...].reshape(SEQ, TILES * 8, PAIR).astype(BF16)

    for n in range(1, SEQ):
        stack_copy(n, seq).wait_send()
        att_copy(n, seq).wait_send()
    for n in range(1, ZH):
        along_z(zs[n]).wait_send()
    for pzh in range(ZH):
        for n in range(1, X):
            along_x(pzh, n).wait_send()
        for px in range(X):
            to_core(px, pzh).wait_send()
    for copy in right_sent:
        copy.wait_send()
    for plane in range(ZH):
        for n in range(1, X):
            tile_copy(plane, n).wait_send()
        pl.when(jnp.logical_not(is_own(plane)))(lambda: tile_copy(plane, 0).wait_send())


def on_device(
    homolog_stack,
    homolog_existing_flags,
    amino_existing_flags,
    asking_weights,
    lookup_weights,
    content_weights,
    sigmoid_weights,
    final_projection,
    former_weights,
    latter_weights,
    couple_projection,
):
    block = SEQS // SEQ
    vmem = pl.BlockSpec(memory_space=pltpu.VMEM)
    hbm = pl.BlockSpec(memory_space=pltpu.HBM)
    dma = pltpu.SemaphoreType.DMA
    operands = (
        homolog_stack,
        homolog_existing_flags[None, :],
        amino_existing_flags[None, :],
        asking_weights, lookup_weights, content_weights, sigmoid_weights, final_projection,
        former_weights.T, latter_weights.T, couple_projection,
    )
    attended, pair = pl.pallas_call(
        kernel,
        out_shape=(
            pltpu.VMEM((SEQ, block, FEATURES), BF16),
            pltpu.VMEM((SEQ, TILES * 8, PAIR), BF16),
        ),
        in_specs=[hbm] * len(operands),
        out_specs=(vmem, vmem),
        scratch_shapes=[pltpu.VMEM(a.shape, a.dtype) for a in operands] + [
            dma((len(operands),)),
            pltpu.VMEM((SEQ, block, FEATURES), BF16),
            pltpu.VMEM((SEQ, block, FEATURES), BF16),
            pltpu.VMEM((SEQ, block, FEATURES), BF16),
            pltpu.VMEM((LEFTS, PROJECTED_DIM, SEQS), BF16),
            pltpu.VMEM((RIGHTS, PROJECTED_DIM, SEQS), BF16),
            pltpu.VMEM((4 * FEATURES, FEATURES), BF16),
            pltpu.VMEM((FEATURES, FEATURES), BF16),
            pltpu.VMEM((2 * PROJECTED_DIM, FEATURES), BF16),
            pltpu.VMEM((PROJECTED_DIM * PROJECTED_DIM, PAIR), BF16),
            pltpu.VMEM((SEQS, SEQS), F32),
            pltpu.VMEM((ZH, 2, PLANE * PROJECTED_DIM, SEQS // 2), F32),
            pltpu.VMEM((ZH, 4, PROJECTED_DIM // 4 * PLANE, RIGHTS * PROJECTED_DIM), F32),
            pltpu.VMEM((ZH, RIGHTS * PLANE, PAIR), F32),
            pltpu.VMEM((TILES, 2, RIGHTS, PAIR), BF16),
            pltpu.VMEM((TILES, 2, RIGHTS, PAIR), BF16),
            pltpu.VMEM((SEQ * TILES * 8, PAIR), F32),
            pltpu.VMEM((ROWS_PICKED, PAIR), F32),
            pltpu.SemaphoreType.REGULAR((ZH,)),
            dma((SEQ,)), dma((SEQ,)), dma((SEQ,)), dma((SEQ,)),
            dma((ZH + 2 * TILES,)), dma((LEFTS,)),
            dma((RIGHTS,)), dma((RIGHTS,)),
            dma((TILES,)), dma((ZH * SEQ,)),
        ],
        compiler_params=pltpu.CompilerParams(
            collective_id=0, has_side_effects=True, vmem_limit_bytes=60 * 2**20
        ),
        name="column_attention_outer_product",
    )(*operands)
    return attended.transpose(1, 0, 2), pair


def solution(mesh):
    in_specs = (P("seq", "dap", None), P(), P(), P(), P(), P(), P(), P(), P(), P(), P())
    out_specs = (P("seq", "dap", None), P("dap", "seq", None))
    return jax.shard_map(
        on_device, mesh=mesh, in_specs=in_specs, out_specs=out_specs, check_vma=False
    )
```

time: 45 us -> 40.5 us (0.900)
  Pallas kernels: 42.8 us -> 38.2 us
    pallas_call x1, Pallas kernels: 42.8 us -> 38.2 us  [on_device(): pl.pallas_call(kernel, out_shape=(pltpu.VMEM((SEQ, block, FEATURES), BF16...]
where the time goes in v4:
time: 40.5 us; the launch traced here: 40.3 us
  Pallas kernels  38.2 us (94%)
  local copies, waits for them, and re-layouts  1.41 us (3%)
  between operations  0.64 us (2%)
    pallas_call x1, Pallas kernels, on_device(): pl.pallas_call(kernel, out_shape=(pltpu.VMEM((SEQ, block, FEATURES), BF16...  38.2 us
    unnamed x2, local copies, waits for them, and re-layouts  1.41 us

profile of v4, /device:TPU:1, one launch (start us, length us, event | category | flops | bytes accessed | tf_op | source)
XLA Modules:
  0.0 40.3 jit_solution(10207472980889015359)
XLA Ops:
  0.6 38.2 %column_attention_outer_product.1 = (bf16[4,64,256]{2,1,0:T(8,128)(2,1)S(1)}, bf16[4,128,128]{2,1,0:T(8,128)(2,1)S(1)}) custom-call(bf16[64,4,256]{2,1,0:T(4,128)(2,1)} %stack_hbm.1, s32[1,256]{1,0:T(1,128)} %bitcast.9, s32[1,512]{1,0:T(1,128)} %bitcast.8, bf16[256,256]{1,0:T(8,128)(2,1)} %asking_hbm.1, bf16[256,256]{1,0:T(8,128)(2,1)} %lookup_hbm.1, ...), custom_call_target="tpu_custom_call" | custom-call | tf_op jit(solution)/shard_map/column_attention_outer_product/pallas_call | solution.py:414
  38.9 0.8 %copy.13 = bf16[64,4,256]{2,1,0:T(4,128)(2,1)} copy(bf16[64,4,256]{2,0,1:T(8,128)(2,1)S(1)} %bitcast.5) | data formatting | bytes 262144
  39.6 0.7 %copy.15 = bf16[4,128,128]{2,1,0:T(8,128)(2,1)} copy(bf16[4,128,128]{2,1,0:T(8,128)(2,1)S(1)} %get-tuple-element.9) | data formatting | bytes 262144

commit v5 on v4

--- a/solution.py
+++ b/solution.py
@@ -38,10 +38,10 @@
     return jnp.where(rows == cols, 1.0, 0.0).astype(BF16)
 
 
-def rescale_rows(values):
-    mean = jnp.mean(values, axis=0, keepdims=True)
+def rescale(values, axis):
+    mean = jnp.mean(values, axis=axis, keepdims=True)
     centred = values - mean
-    variance = jnp.mean(centred * centred, axis=0, keepdims=True)
+    variance = jnp.mean(centred * centred, axis=axis, keepdims=True)
     return centred * lax.rsqrt(variance + 1e-05)
 
 
@@ -53,7 +53,7 @@
     former_ref, latter_ref, couple_ref, local_sems,
     stack_send, stack_all, att_send, left_all, right_all, wt, wt_final, wt_pair, couple, key_mask,
     left_wide, outer, projected, tiles, tiles_in, pair_wide, amino_rows,
-    here_sems, stack_ss, stack_rs, att_ss, att_rs, left_ss, left_rs,
+    here_sems, here_x, here_y, stack_ss, stack_rs, att_ss, att_rs, left_ss, left_rs,
     right_ss, right_rs, tile_ss, tile_rs,
 ):
     dap = lax.axis_index("dap")
@@ -99,10 +99,13 @@
 
     for q in qs[1:]:
         greet((dap, q))
+    def from_first(py):
+        return jnp.minimum(py, Y - py)
+
+    here = from_first(y)
     for py in ys[1:]:
-        greet((dap_of(x, zh, py), seq))
-    for px in xs[1:]:
-        greet((dap_of(px, zh, y), seq))
+        pl.when(from_first(py) >= here)(lambda: greet((dap_of(x, zh, py), seq)))
+    each(x + 1, X, lambda px: greet((dap_of(px, zh, y), seq)))
     each(zh + 1, ZH, lambda pzh: greet((dap_of(x, pzh, y), seq)))
     for copy in local_copies[1:]:
         copy.start()
@@ -115,7 +118,7 @@
     stack_send[...] = dot(by_residue, stack_ref[...].reshape(SEQS, FEATURES)).astype(BF16).reshape(
         SEQ, block, FEATURES)
 
-    pl.semaphore_wait(barrier, SEQ - 1 + X - 1 + Y - 1 + zh)
+    pl.semaphore_wait(barrier, SEQ - 1 + x + 2 * here - lax.div(here, Y // 2) + zh)
 
     def stack_copy(n, slot):
         return copy_to(
@@ -129,12 +132,24 @@
             here_sems.at[zh], inc=1, device_id=(dap_of(x, pzh, y), seq), device_id_type=MESH)
 
     each(0, zh, answer)
+
+    def answer_y(py):
+        pl.semaphore_signal(
+            here_y.at[y], inc=1, device_id=(dap_of(x, zh, py), seq), device_id_type=MESH)
+
+    def answer_x(px):
+        pl.semaphore_signal(
+            here_x.at[x], inc=1, device_id=(dap_of(px, zh, y), seq), device_id_type=MESH)
+
+    for py in ys[1:]:
+        pl.when(from_first(py) < here)(functools.partial(answer_y, py))
+    each(0, x, answer_x)
     stack_all[seq] = stack_send[seq]
 
     for copy in local_copies[1:]:
         copy.wait()
     ident = eye(FEATURES)
-    for n, ref in enumerate((asking_ref, lookup_ref, content_ref, sigmoid_ref)):
+    for n, ref in enumerate((asking_ref, content_ref, sigmoid_ref)):
         wt[n * FEATURES:(n + 1) * FEATURES, :] = dot_t(ident, ref[...]).astype(BF16)
     wt_final[...] = dot_t(ident, final_ref[...]).astype(BF16)
     wt_pair[:PROJECTED_DIM, :] = former_ref[...]
@@ -164,14 +179,14 @@
     for n in range(1, SEQ):
         stack_copy(n, qs[n]).wait_recv()
 
-    incoming = dot_t(ident, stack_all[...].reshape(SEQS, FEATURES))
-    normed = rescale_rows(incoming).astype(BF16)
-    query = (dot(wt[0:256, :], normed) * PER_HEAD_DIM ** (-0.5)).astype(BF16)
-    key_t = dot(wt[256:512, :], normed).astype(BF16)
-    value = dot(wt[512:768, :], normed).astype(BF16)
-    gate = jax.nn.sigmoid(dot(wt[768:1024, :], normed))
-    key = dot_t(ident, key_t).astype(BF16)
-    here = key_mask[...] > 0.5
+    stack = stack_all[...].reshape(SEQS, FEATURES)
+    normed = rescale(stack.astype(F32), 1).astype(BF16)
+    query = (dot_t(wt[0:256, :], normed) * PER_HEAD_DIM ** (-0.5)).astype(BF16)
+    key = dot(normed, lookup_ref[...]).astype(BF16)
+    value = dot_t(wt[256:512, :], normed).astype(BF16)
+    gate = jax.nn.sigmoid(dot_t(wt[512:768, :], normed))
+    incoming = dot_t(ident, stack)
+    unmasked = key_mask[...] > 0.5
     gated = []
     for h in range(HEADS):
         lo = h * PER_HEAD_DIM
@@ -183,7 +198,7 @@
         if after:
             parts.append(jnp.zeros((after, SEQS), BF16))
         scores = dot(key[:, group:group + 128], jnp.concatenate(parts, axis=0))
-        scores = jnp.where(here, scores, -1000000000.0)
+        scores = jnp.where(unmasked, scores, -1000000000.0)
         weights = jnp.exp(scores - jnp.max(scores, axis=0, keepdims=True))
         total = jnp.sum(weights, axis=0, keepdims=True)
         mixed = dot(value[lo:lo + PER_HEAD_DIM], weights.astype(BF16))
@@ -192,7 +207,7 @@
     attended = (incoming + dot(wt_final[...], gated)).astype(BF16)
 
     amino_here = amino_rows[RIGHTS + LEFTS:RIGHTS + LEFTS + 1, :]
-    normed2 = rescale_rows(attended.astype(F32)).astype(BF16)
+    normed2 = rescale(attended.astype(F32), 0).astype(BF16)
     sides = (dot(wt_pair[...], normed2) * (flags * jnp.concatenate([amino_here, amino_here], axis=1))).astype(BF16)
 
     def right_copy(slot, send_sem, device):
@@ -250,8 +265,10 @@
     each(0, zh, lambda pzh: along_z(pzh).start())
     right_all[own] = sides[PROJECTED_DIM:]
     send_right(own, other_l)
-    for n in (1, 7, 2, 6, 3, 5, 4):
+    for n in (4, 3, 5, 2, 6, 1, 7):
+        pl.when(from_first(ys[n]) > here)(lambda: pl.semaphore_wait(here_y.at[ys[n]], 1))
         send_right(own, (dap_of(x, zh, ys[n]), seq))
+    each(x + 1, X, lambda px: pl.semaphore_wait(here_x.at[px], 1))
     spread(zh)
 
     def send_above(pzh):
@@ -274,15 +291,11 @@
     pass_y(3)
     pass_y(5)
     pass_y(4)
-    each(0, zh + 1, take_left)
+    each(0, jnp.minimum(zh + 1, ZH - 1), take_left)
 
     def att_copy(n, slot):
         return copy_to(
             att_send.at[qs[n]], att_ref.at[slot], att_ss.at[n], att_rs.at[slot], (dap, qs[n]))
-
-    for n in range(1, SEQ):
-        att_copy(n, seq).start()
-    att_ref[seq] = att_send[seq]
 
     each(zh + 1, ZH, pass_left)
     for py in range(Y):
@@ -348,7 +361,7 @@
                 projected[plane, pl.ds(n, RIGHTS, stride=PLANE), :] / norm).astype(BF16)
 
     for plane in range(ZH):
-        pl.when(zh < plane)(functools.partial(take_left, plane))
+        pl.when(jnp.logical_or(zh < plane, plane == ZH - 1))(functools.partial(take_left, plane))
         for px in range(X):
             left_of_core(px, plane)
         multiply(plane)
@@ -356,6 +369,10 @@
             tile_copy(plane, n).start()
         pl.when(jnp.logical_not(is_own(plane)))(lambda: tile_copy(plane, 0).start())
         pl.when(is_own(plane))(lambda: own_tile(plane).start())
+        if plane == 0:
+            for n in range(1, SEQ):
+                att_copy(n, seq).start()
+            att_ref[seq] = att_send[seq]
 
     for n in range(1, SEQ):
         att_copy(n, qs[n]).wait_recv()
@@ -426,7 +443,7 @@
             pltpu.VMEM((SEQ, block, FEATURES), BF16),
             pltpu.VMEM((LEFTS, PROJECTED_DIM, SEQS), BF16),
             pltpu.VMEM((RIGHTS, PROJECTED_DIM, SEQS), BF16),
-            pltpu.VMEM((4 * FEATURES, FEATURES), BF16),
+            pltpu.VMEM((3 * FEATURES, FEATURES), BF16),
             pltpu.VMEM((FEATURES, FEATURES), BF16),
             pltpu.VMEM((2 * PROJECTED_DIM, FEATURES), BF16),
             pltpu.VMEM((PROJECTED_DIM * PROJECTED_DIM, PAIR), BF16),
@@ -438,7 +455,7 @@
             pltpu.VMEM((TILES, 2, RIGHTS, PAIR), BF16),
             pltpu.VMEM((SEQ * TILES * 8, PAIR), F32),
             pltpu.VMEM((ROWS_PICKED, PAIR), F32),
-            pltpu.SemaphoreType.REGULAR((ZH,)),
+            pltpu.SemaphoreType.REGULAR((ZH,)), pltpu.SemaphoreType.REGULAR((X,)), pltpu.SemaphoreType.REGULAR((Y,)),
             dma((SEQ,)), dma((SEQ,)), dma((SEQ,)), dma((SEQ,)),
             dma((ZH + 2 * TILES,)), dma((LEFTS,)),
             dma((RIGHTS,)), dma((RIGHTS,)),

time: 40.5 us -> 39.2 us (0.968)
  Pallas kernels: 38.2 us -> 36.9 us
    pallas_call x1, Pallas kernels: 38.2 us -> 36.9 us  [on_device(): pl.pallas_call(kernel, out_shape=(pltpu.VMEM((SEQ, block, FEATURES), BF16...]
where the time goes in v5:
time: 39.2 us; the launch traced here: 38.9 us
  Pallas kernels  36.9 us (94%)
  local copies, waits for them, and re-layouts  1.41 us (4%)
  between operations  0.64 us (2%)
    pallas_call x1, Pallas kernels, on_device(): pl.pallas_call(kernel, out_shape=(pltpu.VMEM((SEQ, block, FEATURES), BF16...  36.9 us
    unnamed x2, local copies, waits for them, and re-layouts  1.41 us

profile of v5, /device:TPU:1, one launch (start us, length us, event | category | flops | bytes accessed | tf_op | source)
XLA Modules:
  0.0 38.9 jit_solution(2946805540948248398)
XLA Ops:
  0.6 36.9 %column_attention_outer_product.1 = (bf16[4,64,256]{2,1,0:T(8,128)(2,1)S(1)}, bf16[4,128,128]{2,1,0:T(8,128)(2,1)S(1)}) custom-call(bf16[64,4,256]{2,1,0:T(4,128)(2,1)} %stack_hbm.1, s32[1,256]{1,0:T(1,128)} %bitcast.9, s32[1,512]{1,0:T(1,128)} %bitcast.8, bf16[256,256]{1,0:T(8,128)(2,1)} %asking_hbm.1, bf16[256,256]{1,0:T(8,128)(2,1)} %lookup_hbm.1, ...), custom_call_target="tpu_custom_call" | custom-call | tf_op jit(solution)/shard_map/column_attention_outer_product/pallas_call | solution.py:431
  37.5 0.8 %copy.13 = bf16[64,4,256]{2,1,0:T(4,128)(2,1)} copy(bf16[64,4,256]{2,0,1:T(8,128)(2,1)S(1)} %bitcast.5) | data formatting | bytes 262144
  38.3 0.7 %copy.15 = bf16[4,128,128]{2,1,0:T(8,128)(2,1)} copy(bf16[4,128,128]{2,1,0:T(8,128)(2,1)S(1)} %get-tuple-element.9) | data formatting | bytes 262144

commit v6 on v5

--- a/solution.py
+++ b/solution.py
@@ -265,11 +265,12 @@
     each(0, zh, lambda pzh: along_z(pzh).start())
     right_all[own] = sides[PROJECTED_DIM:]
     send_right(own, other_l)
-    for n in (4, 3, 5, 2, 6, 1, 7):
+    for n in (1, 7, 2, 6, 3, 5, 4):
         pl.when(from_first(ys[n]) > here)(lambda: pl.semaphore_wait(here_y.at[ys[n]], 1))
         send_right(own, (dap_of(x, zh, ys[n]), seq))
     each(x + 1, X, lambda px: pl.semaphore_wait(here_x.at[px], 1))
     spread(zh)
+    each(0, zh, pass_left)
 
     def send_above(pzh):
         pl.semaphore_wait(here_sems.at[pzh], 1)
@@ -285,7 +286,6 @@
     att_send[...] = dot_t(ident, attended).astype(BF16).reshape(SEQ, SEQS // SEQ, FEATURES)
     pass_y(1)
     pass_y(7)
-    each(0, zh, pass_left)
     pass_y(2)
     pass_y(6)
     pass_y(3)
@@ -298,8 +298,6 @@
             att_send.at[qs[n]], att_ref.at[slot], att_ss.at[n], att_rs.at[slot], (dap, qs[n]))
 
     each(zh + 1, ZH, pass_left)
-    for py in range(Y):
-        right_arrived(py * 2 + 1 - l)
 
     def left_of_core(px, pzh):
         slot = left_slot(1 - c, px, pzh)
@@ -330,30 +328,32 @@
         lefts = left_all[first:first + PLANE].reshape(PLANE * PROJECTED_DIM, SEQS).astype(F32)
         for half in range(2):
             left_wide[plane, half] = lefts[:, half * 128:(half + 1) * 128]
-        for k in range(4):
-            left_k = jnp.concatenate(
+        turned = [
+            jnp.concatenate(
                 [jnp.concatenate(
                     [left_wide[plane, half, pl.ds(4 * g + k, PLANE, stride=PROJECTED_DIM), :]
                      for half in range(2)], axis=1)
                  for g in range(groups)], axis=0).astype(BF16)
+            for k in range(4)
+        ]
+        if plane == 0:
+            for py in range(Y):
+                right_arrived(py * 2 + 1 - l)
+        for k in range(4):
             blocks = [right_all[4 * turn + (m - k) % 4] for turn in range(turns) for m in range(4)]
-            outer[plane, k] = dot_t(left_k, jnp.concatenate(blocks, axis=0))
-        for a in range(4):
-            flat = []
-            for turn in range(turns):
-                cols = slice(turn * 128, (turn + 1) * 128)
-                chosen = outer[plane, (3 - a) % 4, :, cols]
+            outer[plane, k] = dot_t(turned[k], jnp.concatenate(blocks, axis=0))
+        flat = []
+        for turn in range(turns):
+            lanes = slice(turn * 128, (turn + 1) * 128)
+            for a in range(4):
+                chosen = outer[plane, (3 - a) % 4, :, lanes]
                 for m in range(3):
-                    chosen = jnp.where(lane_block == m, outer[plane, (m - a) % 4, :, cols], chosen)
+                    chosen = jnp.where(lane_block == m, outer[plane, (m - a) % 4, :, lanes], chosen)
+                if a:
+                    chosen = pltpu.roll(chosen, 128 - a * PROJECTED_DIM, 1)
                 flat.append(jnp.concatenate(
                     [chosen[g * PLANE:(g + 1) * PLANE] for g in range(groups)], axis=1))
-            rows_a = jnp.concatenate(
-                [couple[(4 * g + (m - a) % 4) * PROJECTED_DIM:(4 * g + (m - a) % 4 + 1) * PROJECTED_DIM, :]
-                 for g in range(groups) for m in range(4)], axis=0)
-            result = dot(jnp.concatenate(flat, axis=0).astype(BF16), rows_a)
-            for turn in range(turns):
-                at = (turn * 4 + a) * PLANE
-                projected[plane, at:at + PLANE, :] = result[turn * PLANE:(turn + 1) * PLANE]
+        projected[plane] = dot(jnp.concatenate(flat, axis=0).astype(BF16), couple[...])
         for n in range(PLANE):
             i = RIGHTS + first + n
             norm = jnp.maximum(norm_cols * amino_rows[i:i + 1, :], 1.0)

time: 39.2 us -> 38.5 us (0.982)
  Pallas kernels: 36.9 us -> 36.3 us
    pallas_call x1, Pallas kernels: 36.9 us -> 36.3 us  [on_device(): pl.pallas_call(kernel, out_shape=(pltpu.VMEM((SEQ, block, FEATURES), BF16...]
where the time goes in v6:
time: 38.5 us; the launch traced here: 38.3 us
  Pallas kernels  36.3 us (94%)
  local copies, waits for them, and re-layouts  1.41 us (4%)
  between operations  0.64 us (2%)
    pallas_call x1, Pallas kernels, on_device(): pl.pallas_call(kernel, out_shape=(pltpu.VMEM((SEQ, block, FEATURES), BF16...  36.3 us
    unnamed x2, local copies, waits for them, and re-layouts  1.41 us

profile of v6, /device:TPU:1, one launch (start us, length us, event | category | flops | bytes accessed | tf_op | source)
XLA Modules:
  0.0 38.3 jit_solution(332980525081421552)
XLA Ops:
  0.6 36.3 %column_attention_outer_product.1 = (bf16[4,64,256]{2,1,0:T(8,128)(2,1)S(1)}, bf16[4,128,128]{2,1,0:T(8,128)(2,1)S(1)}) custom-call(bf16[64,4,256]{2,1,0:T(4,128)(2,1)} %stack_hbm.1, s32[1,256]{1,0:T(1,128)} %bitcast.9, s32[1,512]{1,0:T(1,128)} %bitcast.8, bf16[256,256]{1,0:T(8,128)(2,1)} %asking_hbm.1, bf16[256,256]{1,0:T(8,128)(2,1)} %lookup_hbm.1, ...), custom_call_target="tpu_custom_call" | custom-call | tf_op jit(solution)/shard_map/column_attention_outer_product/pallas_call | solution.py:431
  36.9 0.8 %copy.13 = bf16[64,4,256]{2,1,0:T(4,128)(2,1)} copy(bf16[64,4,256]{2,0,1:T(8,128)(2,1)S(1)} %bitcast.5) | data formatting | bytes 262144
  37.7 0.7 %copy.15 = bf16[4,128,128]{2,1,0:T(8,128)(2,1)} copy(bf16[4,128,128]{2,1,0:T(8,128)(2,1)S(1)} %get-tuple-element.9) | data formatting | bytes 262144

commit v7 on v6

--- a/solution.py
+++ b/solution.py
@@ -269,8 +269,8 @@
         pl.when(from_first(ys[n]) > here)(lambda: pl.semaphore_wait(here_y.at[ys[n]], 1))
         send_right(own, (dap_of(x, zh, ys[n]), seq))
     each(x + 1, X, lambda px: pl.semaphore_wait(here_x.at[px], 1))
+    each(0, zh, pass_left)
     spread(zh)
-    each(0, zh, pass_left)
 
     def send_above(pzh):
         pl.semaphore_wait(here_sems.at[pzh], 1)

time: 38.5 us -> 38.5 us (level)
  no operation moved by 1% of the time
where the time goes in v7:
time: 38.5 us; the launch traced here: 38.3 us
  Pallas kernels  36.3 us (94%)
  local copies, waits for them, and re-layouts  1.41 us (4%)
  between operations  0.64 us (2%)
    pallas_call x1, Pallas kernels, on_device(): pl.pallas_call(kernel, out_shape=(pltpu.VMEM((SEQ, block, FEATURES), BF16...  36.3 us
    unnamed x2, local copies, waits for them, and re-layouts  1.41 us

profile of v7, /device:TPU:1, one launch (start us, length us, event | category | flops | bytes accessed | tf_op | source)
XLA Modules:
  0.0 38.3 jit_solution(12831019986456136799)
XLA Ops:
  0.6 36.3 %column_attention_outer_product.1 = (bf16[4,64,256]{2,1,0:T(8,128)(2,1)S(1)}, bf16[4,128,128]{2,1,0:T(8,128)(2,1)S(1)}) custom-call(bf16[64,4,256]{2,1,0:T(4,128)(2,1)} %stack_hbm.1, s32[1,256]{1,0:T(1,128)} %bitcast.9, s32[1,512]{1,0:T(1,128)} %bitcast.8, bf16[256,256]{1,0:T(8,128)(2,1)} %asking_hbm.1, bf16[256,256]{1,0:T(8,128)(2,1)} %lookup_hbm.1, ...), custom_call_target="tpu_custom_call" | custom-call | tf_op jit(solution)/shard_map/column_attention_outer_product/pallas_call | solution.py:431
  36.9 0.8 %copy.13 = bf16[64,4,256]{2,1,0:T(4,128)(2,1)} copy(bf16[64,4,256]{2,0,1:T(8,128)(2,1)S(1)} %bitcast.5) | data formatting | bytes 262144
  37.7 0.7 %copy.15 = bf16[4,128,128]{2,1,0:T(8,128)(2,1)} copy(bf16[4,128,128]{2,1,0:T(8,128)(2,1)S(1)} %get-tuple-element.9) | data formatting | bytes 262144
